TPU v7x, 512 devices: a whole 4x4x16 slice. The times are simulated.
512 devices in a mesh: prow: 16 (over z), pcol: 32 (over y, x, core).
Axes of the slice: x: 4, y: 4, z: 16, core: 2. Of those that a mesh axis runs over, the one named last changes fastest.
Arguments:
- matrix: float32 [12288, 24576], P('prow', 'pcol'), may hold values from -6 to 6
- panel: float32 [12288, 512], P('prow', 'pcol'), may hold values from -0.25 to 0.25
- l_inverse: float32 [512, 512], replicated, as said below
- touched: int32 [1024], replicated, may hold values from 0 to 12287, as said below
- anchor: int32 [1024], replicated, may hold values from 0 to 12287, as said below
Outputs:
- updated: float32 [12288, 24576], P('prow', 'pcol')
Inputs may be any that keep to these rules, and one draw needn't show every extreme that they name: touched[k] = k for k below 512; its last 512 entries are the pivot rows of the panel's columns, each at least its column's index; equal entries of touched have equal entries of anchor. anchor is the row ordering of the panel's interchanges, applied in turn, read at the positions in touched: it permutes the set of touched positions. l_inverse is unit lower triangular.
All inputs are finite; a program needn't handle non-finite values.
Results may differ from a plain program's by a relative error of at most 0.000057.
Values sent between devices are 32-bit elements; how exact they have to be, the bound alone decides.
A program may use at most 64 MiB of HBM per device.

v0:
```python
import jax
import jax.numpy as jnp
from jax import lax
from jax.sharding import PartitionSpec as P


def body(matrix, panel, l_inverse, touched, anchor):
    row_dev = matrix.shape[0]
    panel_width = l_inverse.shape[0]
    offset = lax.axis_index("prow") * row_dev
    local_idx = anchor - offset
    is_owned = (local_idx >= 0) & (local_idx < row_dev)
    taken = matrix[jnp.clip(local_idx, 0, row_dev - 1)]
    picked = jnp.where(is_owned[:, None], taken, jnp.zeros_like(taken))
    moved_rows = lax.psum(picked, "prow")
    upper_rows = jnp.dot(
        l_inverse,
        moved_rows[:panel_width],
        precision=lax.Precision.HIGHEST,
        preferred_element_type=jnp.float32,
    )
    target_idx = touched - offset
    target_idx = jnp.where((target_idx >= 0) & (target_idx < row_dev), target_idx, row_dev)
    permuted = matrix.at[target_idx].set(moved_rows, mode="drop")
    return permuted - jnp.dot(
        lax.all_gather(panel, "pcol", axis=1, tiled=True),
        upper_rows,
        precision=lax.Precision.HIGHEST,
        preferred_element_type=jnp.float32,
    )


def solution(mesh):
    in_specs = (P("prow", "pcol"), P("prow", "pcol"), P(), P(), P())
    out_specs = P("prow", "pcol")
    return jax.shard_map(body, mesh=mesh, in_specs=in_specs, out_specs=out_specs, check_vma=False)
```

profile of v0, /device:TPU:6, one launch (start us, length us, event | category | flops | bytes accessed | tf_op | source)
XLA Modules:
  0.0 207.9 jit_solution(11141209007732240128)
XLA Ops:
  7.4 0.0 copy-start
  7.4 0.0 copy-start.2
  7.4 0.0 all-reduce.2.cloned.1.call-start
  7.4 1.8 copy.11
  9.1 0.0 copy-done.2
  9.2 5.2 %gather_fusion = f32[1024,768]{1,0:T(8,128)} fusion(f32[768,768]{1,0:T(8,128)S(1)} %copy.11, s32[1024]{0:T(1024)S(1)} %fusion.2), kind=kCustom, calls=%fused_computation | custom fusion | bytes 6295552 | tf_op jit(solution)/shard_map/gather | solution.py:13
  14.4 3.8 %broadcast_select_fusion = f32[1024,768]{1,0:T(8,128)} fusion(f32[1024,768]{1,0:T(8,128)} %gather_fusion, pred[1024]{0:T(1024)(128)(4,1)S(1)} %compare_and_fusion), kind=kLoop, calls=%fused_computation.5 | loop fusion | flops 786432 | bytes 6292480 | tf_op jit(solution)/shard_map/jit(_where)/select_n | solution.py:14
  18.3 0.0 copy-start.3
  18.3 0.0 all-reduce.2.cloned.1.call-update
  18.3 0.0 all-gather.2.cloned.1.call-start
  18.3 0.5 all-gather.2.cloned.1.call-update
  18.9 0.1 copy-done.3
  18.9 154.8 %all-reduce.2.cloned.1.call-done = f32[1024,768]{1,0:T(8,128)} async-done(((f32[1024,768]{1,0:T(8,128)}), f32[1024,768]{1,0:T(8,128)}) %all-reduce.2.cloned.1.call-update) | async-done | bytes 3145744 | tf_op jit(solution)/shard_map/psum | solution.py:15
  173.7 6.7 %scatter_fusion = f32[768,768]{1,0:T(8,128)S(1)} fusion(f32[768,768]{1,0:T(8,128)S(1)} %copy.11, s32[1024]{0:T(1024)S(1)} %compare_select_fusion.1, f32[1024,768]{1,0:T(8,128)} %all-reduce.2.cloned.1.call-done), kind=kCustom, calls=%fused_computation.1 | custom fusion | bytes 9441280 | tf_op jit(solution)/shard_map/scatter | solution.py:24
  180.4 2.0 copy.6
  182.3 0.0 copy-done
  182.3 0.0 copy-start.1
  182.3 7.8 %fusion = f32[768,512]{1,0:T(8,128)} fusion(f32[512,512]{1,0:T(8,128)S(1)} %copy-done, f32[1024,768]{1,0:T(8,128)} %all-reduce.2.cloned.1.call-done), kind=kOutput, calls=%fused_computation.3 | convolution fusion | flops 2415919104 | bytes 4194304 | tf_op jit(solution)/shard_map/dot_general | solution.py:16
  190.1 0.0 all-gather.2.cloned.1.call-done
  190.1 0.0 copy-done.1
  190.1 7.3 %bitcast_subtract_fusion = f32[768,768]{0,1:T(8,128)} fusion(f32[768,768]{0,1:T(8,128)S(1)} %copy-done.1, f32[768,512]{1,0:T(8,128)} %fusion, f32[768,512]{0,1:T(8,128)} %all-gather.2.cloned.1.call-done), kind=kOutput, calls=%fused_computation.2 | convolution fusion | flops 3624468480 | bytes 7864320 | tf_op jit(solution)/shard_map/dot_general | solution.py:25
  197.4 3.0 %copy.7 = f32[768,768]{1,0:T(8,128)} copy(f32[768,768]{0,1:T(8,128)} %bitcast_subtract_fusion) | data formatting | bytes 4718592 | tf_op jit(solution)/shard_map/sub | solution.py:25
  (3 shorter events, 0.0 us)
Async XLA Ops:
  7.4 175.0 %copy-start = (f32[512,512]{1,0:T(8,128)S(1)}, f32[512,512]{1,0:T(8,128)}, u32[]{:S(2)}) copy-start(f32[512,512]{1,0:T(8,128)} %param.7) | copy-start | bytes 3145732
  7.4 1.8 copy-start.2
  7.4 166.3 %all-reduce.2.cloned.1.call-start = ((), (), s32[]{:S(2)}) async-start(), calls=%async_computation | async-start | bytes 6291456 | tf_op jit(solution)/shard_map/psum | solution.py:15
  18.3 0.7 copy-start.3
  18.3 171.8 %all-gather.2.cloned.1.call-start = ((), (), s32[]{:S(2)}) async-start(), calls=%async_computation.1 | async-start | bytes 1622016 | tf_op jit(solution)/shard_map/all_gather | solution.py:26
  182.3 7.8 %copy-start.1 = (f32[768,768]{0,1:T(8,128)S(1)}, f32[768,768]{0,1:T(8,128)}, u32[]{:S(2)}) copy-start(f32[768,768]{0,1:T(8,128)} %copy.6) | copy-start | bytes 7077892
Sparse Core Ops, SparseCore 0:
  18.4 155.2 all-reduce.1
Sparse Core Ops, SparseCore 1:
  21.9 62.6 all-gather.1
where the time goes:
time: 208 us
  waiting for transfers between devices  155 us (75%)
  local copies, waits for them, and re-layouts  18.8 us (9%)
  matrix products  15 us (7%)
  between operations  14.9 us (7%)
  other arithmetic  3.87 us (2%)
    psum x1, waiting for transfers between devices, body(): moved_rows = lax.psum(picked, 'prow')  155 us
    scatter x2, local copies, waits for them, and re-layouts, body(): permuted = matrix.at[target_idx].set(moved_rows, mode='drop')  8.64 us
    dot_general x1, matrix products, body(): jnp.dot(l_inverse, moved_rows[:panel_width], precision=lax.Precision.HIGH...  7.77 us
    dot_general x1, matrix products, body(): jnp.dot(lax.all_gather(panel, 'pcol', axis=1, tiled=True), upper_rows, pr...  7.27 us
    gather x1, local copies, waits for them, and re-layouts, body(): taken = matrix[jnp.clip(local_idx, 0, row_dev - 1)]  5.24 us
  transfers between devices with their start and end apart: 2, of which 1 were waited for; matrix products, arithmetic and copies ran while one was open for 8% of the time, Pallas kernels for 0%

commit v1 on v0

v1 whole, which is shorter than its diff:
```python
import functools

import jax
import jax.numpy as jnp
from jax import lax
from jax.experimental import pallas as pl
from jax.experimental.pallas import tpu as pltpu
from jax.sharding import PartitionSpec as P

MESH = pl.DeviceIdType.MESH
NZ = 16
CH = 32
HALF = 16
NSTEP = 10
NB = NZ * CH
F32, BF16 = jnp.float32, jnp.bfloat16


def reach(j):
    return (j + 1) // 2 + 2


def split(x):
    hi = x.astype(BF16)
    return hi, (x - hi.astype(F32)).astype(BF16)


def dot(a, b, ca=1):
    return lax.dot_general(a, b, (((ca,), (0,)), ((), ())), preferred_element_type=F32)


def kernel(
    shape, qsrc, ssrc, inv_ref, tgt_ref, mat, pan, linv, out,
    contrib, left1, right1, left2, right2, q, t, pall, lhi, llo, whi, wlo, hot,
    p_send, p_recv, s_send, s_recv, pan_send, pan_recv,
):
    ny, nx, nc = shape
    rows, cols = mat.shape
    z = lax.axis_index("prow")
    w = lax.axis_index("pcol")
    core, x, y = w % nc, (w // nc) % nx, w // (nc * nx)
    off = z * rows
    up, down = (z + 1) % NZ, (z + NZ - 1) % NZ
    dist = (z, (NZ - z) % NZ)
    nxt = ({"prow": up}, {"prow": down})

    def pcol(yy, xx, cc):
        return {"pcol": (yy * nx + xx) * nc + cc}

    xpart = [pcol(y, (x + d) % nx, core) for d in range(1, nx)]
    ypart = [pcol((y + d) % ny, x, core) for d in range(1, ny)]
    cpart = [pcol(y, x, 1 - core)] if nc == 2 else []
    partners = list(nxt) + xpart + ypart + cpart

    t[...] = jnp.zeros_like(t)

    barrier = pltpu.get_barrier_semaphore()
    for dev in partners:
        pl.semaphore_signal(barrier, inc=1, device_id=dev, device_id_type=MESH)
    pl.semaphore_wait(barrier, len(partners))

    def remote(src, dst, ss, rs, dev):
        return pltpu.make_async_remote_copy(
            src_ref=src, dst_ref=dst, send_sem=ss, recv_sem=rs, device_id=dev, device_id_type=MESH
        )

    mine = y * nx + x

    def pan_x(i):
        return remote(pan, pall.at[mine, core], pan_send.at[i], pan_recv.at[i], xpart[i])

    def pan_y(i):
        rowset = pall.at[pl.ds(y * nx, nx), core]
        return remote(rowset, rowset, pan_send.at[nx - 1 + i], pan_recv.at[nx - 1 + i], ypart[i])

    def pan_c():
        k = nx + ny - 2
        return remote(pall.at[:, core], pall.at[:, core], pan_send.at[k], pan_recv.at[k], cpart[0])

    def home(d, k):
        if k == 0:
            src = contrib.at[pl.ds(112, HALF)] if d == 0 else contrib.at[pl.ds(0, HALF)]
            dst = (left1, right1)[d]
        else:
            src = contrib.at[pl.ds(80, CH)] if d == 0 else contrib.at[pl.ds(16, CH)]
            dst = (left2, right2)[d]
        i = 2 * k + d
        return remote(src, dst, p_send.at[i], p_recv.at[i], nxt[d])

    def gather(d, k):
        src, dst = ((5 - k) % NZ, (4 - k) % NZ) if d == 0 else (3 + k, 4 + k)
        part = pl.ds(0, CH) if k < 8 else pl.ds(HALF * d, HALF)
        i = 4 + 2 * (k - 1) + d
        return remote(q.at[src, part], q.at[dst, part], p_send.at[i], p_recv.at[i], nxt[d])

    def take_rows(first, count):
        def one(i, _):
            r = first + i
            li = qsrc[80 + r] - off
            row = mat[pl.ds(jnp.clip(li, 0, rows - 1), 1), :]
            contrib[pl.ds(r, 1), :] = jnp.where((li >= 0) & (li < rows), row, 0.0)
            return 0

        lax.fori_loop(0, count, one, 0, unroll=4)

    def piece(d, j):
        return j if d == 0 else 31 - j

    def scatter(d, j):
        c = piece(d, j)
        return remote(t.at[c], t.at[c], s_send.at[d, j], s_recv.at[d, j], nxt[d])

    def pieces(b):
        first = 15 - 2 * b - jnp.minimum(b, 2)
        return [(first - u, (b >= 0) & (b <= 6) & ((u < 2) | (b < 2))) for u in range(3)]

    def fill(b):
        if b > 6:
            return
        first, count = 15 - 2 * b - min(b, 2), 3 if b < 2 else 2

        @pl.when(z == 0)
        def _():
            for d in (0, 1):
                base = HALF * (first - count + 1 if d == 0 else 31 - first)

                def one(i, _):
                    r = base + i
                    row = mat[pl.ds(jnp.clip(ssrc[r], 0, rows - 1), 1), :]
                    t[r // HALF, pl.ds(r % HALF, 1), :] = row
                    return 0

                lax.fori_loop(0, HALF * count, one, 0, unroll=4)

    def pass_on(step):
        for d in (0, 1):
            for j, valid in pieces(step - dist[d]):
                j = jnp.clip(j, 0, 15)

                @pl.when(valid & (dist[d] >= 1) & (dist[d] <= reach(j)))
                def _():
                    scatter(d, j).wait_recv()

                if step < NSTEP:

                    @pl.when(valid & (dist[d] < reach(j)))
                    def _():
                        scatter(d, j).start()

    def order():
        kk = lax.broadcasted_iota(jnp.int32, (NB, NB), 0)
        perm = (kk == inv_ref[...]).astype(F32).astype(BF16)
        hi, lo = split(linv[...])
        lhi[...] = dot(hi, perm).astype(BF16)
        llo[...] = dot(lo, perm).astype(BF16)

    def base():
        for r in range(0, rows, 256):
            qq = lax.broadcasted_iota(jnp.int32, (256, NB), 0) + r
            hit = (qq + off == tgt_ref[...]).astype(F32)
            hot[pl.ds(r, 256), :] = hit.astype(BF16)
            gone = jnp.max(hit, axis=1, keepdims=True) > 0.0
            top = (lax.broadcasted_iota(jnp.int32, (256, 1), 0) + r < NB) & (z == 0)
            out[pl.ds(r, 256), :] = jnp.where(gone | top, 0.0, mat[pl.ds(r, 256), :])

    def weights(r):
        a = pall[...].reshape(NB, rows)[:, r:r + 256]
        ahi, alo = split(a)
        acc = dot(ahi, lhi[...], 0) + dot(ahi, llo[...], 0) + dot(alo, lhi[...], 0)
        qq = lax.broadcasted_iota(jnp.int32, (256, NB), 0) + r
        own = (qq == inv_ref[...]) & (z == 0)
        acc = acc - own.astype(F32)
        hi, lo = split(acc)
        whi[pl.ds(r, 256), :] = hi
        wlo[pl.ds(r, 256), :] = lo

    def update(k, c):
        qhi, qlo = split(q[k // CH:k // CH + 8, :, c:c + 256].reshape(256, 256))
        a, b = whi[:, k:k + 256], wlo[:, k:k + 256]
        out[:, c:c + 256] -= dot(a, qhi) + dot(a, qlo) + dot(b, qhi)

    def moved(c):
        thi, tlo = split(t[:, :, c:c + 256].reshape(NB, 256))
        out[:, c:c + 256] += dot(hot[...], thi) + dot(hot[...], tlo)

    stripes = list(range(0, cols, 256))

    for i in range(nx - 1):
        pan_x(i).start()
    take_rows(0, HALF)
    take_rows(112, HALF)
    home(0, 0).start()
    home(1, 0).start()
    fill(0)
    pass_on(0)
    take_rows(16, CH)
    take_rows(80, CH)
    pall[mine, core] = pan[...]

    home(0, 0).wait_recv()
    contrib[pl.ds(80, HALF), :] += left1[...]
    home(0, 1).start()
    home(1, 0).wait_recv()
    contrib[pl.ds(32, HALF), :] += right1[...]
    home(1, 1).start()
    fill(1)
    pass_on(1)
    take_rows(48, CH)
    fill(2)
    for i in range(nx - 1):
        pan_x(i).wait_recv()
    for i in range(ny - 1):
        pan_y(i).start()

    home(0, 1).wait_recv()
    home(1, 1).wait_recv()
    q[4] = contrib[pl.ds(48, CH), :] + left2[...] + right2[...]
    for k in range(1, 9):
        if k > 1:
            gather(0, k - 1).wait_recv()
        gather(0, k).start()
        if k > 1:
            gather(1, k - 1).wait_recv()
        gather(1, k).start()
        pass_on(1 + k)
        fill(2 + k)
        if k == 1:
            order()
        if k == 2:
            base()
        if k == 3:
            for i in range(ny - 1):
                pan_y(i).wait_recv()
            if cpart:
                pan_c().start()
        if k == 4:
            if cpart:
                pan_c().wait_recv()
            for r in range(0, rows, 256):
                weights(r)
        if k >= 5 and k - 5 < len(stripes):
            update(0, stripes[k - 5])
    gather(0, 8).wait_recv()
    gather(1, 8).wait_recv()
    pass_on(NSTEP)
    for c in stripes:
        moved(c)
        update(256, c)

    for d in (0, 1):
        home(d, 0).wait_send()
        home(d, 1).wait_send()
        for k in range(1, 9):
            gather(d, k).wait_send()

        def sent(j, _):
            @pl.when(dist[d] < reach(j))
            def _():
                scatter(d, j).wait_send()

            return 0

        lax.fori_loop(0, 16, sent, 0)
    for i in range(nx - 1):
        pan_x(i).wait_send()
    for i in range(ny - 1):
        pan_y(i).wait_send()
    if cpart:
        pan_c().wait_send()


def plan(touched, anchor, rows, z):
    idx = jnp.arange(NB, dtype=jnp.int32)
    src, owner = anchor[:NB], anchor[:NB] // rows
    tgt, top = touched[NB:], anchor[NB:]
    dest = tgt // rows
    again = jnp.any((tgt[None, :] == tgt[:, None]) & (idx[None, :] < idx[:, None]), axis=1)
    tgt = jnp.where(again | (tgt < NB), -1, tgt)

    def rank(group):
        key = group * NB + idx
        return jnp.sum((key[None, :] < key[:, None]).astype(jnp.int32), axis=1)

    def place(pos, values):
        return jnp.sum(jnp.where(pos[:, None] == idx[None, :], values[:, None], 0), axis=0)

    r, s = rank(owner), rank(dest)
    away = (owner - r // CH + 8) % NZ - 8
    late = r % CH >= HALF
    fits = (jnp.abs(away) <= 1) | ((away == -2) & ~late) | ((away == 2) & late)
    hops = jnp.where(s < NB // 2, dest, NZ - dest)
    near = jnp.where(s < NB // 2, s, NB - 1 - s) // HALF
    fits &= (tgt < rows) | (hops <= reach(near))
    here = (r - CH * z + 4 * CH) % NB
    return jnp.all(fits), place(here, src), place(s, top), place(here, idx), place(s, tgt)


def plain(matrix, panel_t, l_inverse, touched, anchor):
    rows = matrix.shape[0]
    offset = lax.axis_index("prow") * rows
    local = anchor - offset
    owned = (local >= 0) & (local < rows)
    picked = jnp.where(owned[:, None], matrix[jnp.clip(local, 0, rows - 1)], 0.0)

    def ring(axis, init):
        n = lax.axis_size(axis)
        pairs = [(i, (i + 1) % n) for i in range(n)]
        return n, lambda v: lax.ppermute(v, axis, pairs), init

    n, shift, _ = ring("prow", None)

    def add(_, carry):
        part, total = carry
        part = shift(part)
        return part, total + part

    _, moved = lax.fori_loop(0, n - 1, add, (picked, picked))
    m, shift_p, _ = ring("pcol", None)
    me = lax.axis_index("pcol")
    wide = jnp.zeros((m,) + panel_t.shape, panel_t.dtype).at[me].set(panel_t)

    def put(i, carry):
        part, whole = carry
        part = shift_p(part)
        return part, lax.dynamic_update_index_in_dim(whole, part, (me - 1 - i) % m, 0)

    _, wide = lax.fori_loop(0, m - 1, put, (panel_t, wide))
    high = functools.partial(jnp.dot, precision=lax.Precision.HIGHEST, preferred_element_type=F32)
    upper = high(l_inverse, moved[:NB])
    target = touched - offset
    target = jnp.where((target >= 0) & (target < rows), target, rows)
    permuted = matrix.at[target].set(moved, mode="drop")
    return permuted - high(wide.reshape(NB, rows).T, upper)


def fast(shape, matrix, panel_t, l_inverse, qsrc, ssrc, inv, tgt):
    rows, cols = matrix.shape
    ny, nx, nc = shape
    vmem, smem = pl.BlockSpec(memory_space=pltpu.VMEM), pl.BlockSpec(memory_space=pltpu.SMEM)
    npan = max(nx + ny - 1, 1)
    dma = pltpu.SemaphoreType.DMA
    return pl.pallas_call(
        functools.partial(kernel, shape),
        out_shape=jax.ShapeDtypeStruct((rows, cols), F32),
        in_specs=[smem, smem] + [vmem] * 5,
        out_specs=vmem,
        scratch_shapes=[
            pltpu.VMEM((128, cols), F32),
            pltpu.VMEM((HALF, cols), F32),
            pltpu.VMEM((HALF, cols), F32),
            pltpu.VMEM((CH, cols), F32),
            pltpu.VMEM((CH, cols), F32),
            pltpu.VMEM((NZ, CH, cols), F32),
            pltpu.VMEM((32, HALF, cols), F32),
            pltpu.VMEM((ny * nx, nc, panel_t.shape[0], rows), F32),
            pltpu.VMEM((NB, NB), BF16),
            pltpu.VMEM((NB, NB), BF16),
            pltpu.VMEM((rows, NB), BF16),
            pltpu.VMEM((rows, NB), BF16),
            pltpu.VMEM((rows, NB), BF16),
            dma((20,)), dma((20,)), dma((2, 16)), dma((2, 16)), dma((npan,)), dma((npan,)),
        ],
        compiler_params=pltpu.CompilerParams(
            collective_id=0, has_side_effects=True, vmem_limit_bytes=48 * 2**20
        ),
    )(qsrc, ssrc, inv.reshape(1, NB), tgt.reshape(1, NB), matrix, panel_t, l_inverse)


def body(shape, matrix, panel, l_inverse, touched, anchor):
    z = lax.axis_index("prow")
    fits, qsrc, ssrc, inv, tgt = plan(touched, anchor, matrix.shape[0], z)
    panel_t = panel.T
    return lax.cond(
        fits,
        lambda: fast(shape, matrix, panel_t, l_inverse, qsrc, ssrc, inv, tgt),
        lambda: plain(matrix, panel_t, l_inverse, touched, anchor),
    )


def solution(mesh):
    n = mesh.shape["pcol"]
    shape = (4, 4, 2) if n == 32 else (1, n, 1)
    in_specs = (P("prow", "pcol"), P("prow", "pcol"), P(), P(), P())
    return jax.shard_map(
        functools.partial(body, shape), mesh=mesh, in_specs=in_specs, out_specs=P("prow", "pcol"), check_vma=False
    )
```

time: 208 us -> 71.2 us (0.34)
  waiting for transfers between devices: 155 us -> 0 us
  Pallas kernels: 0 us -> 61.7 us
  matrix products: 15 us -> 0 us
  between operations: 14.9 us -> 0.7 us
  local copies, waits for them, and re-layouts: 18.8 us -> 5.24 us
    psum x1 -> x0, waiting for transfers between devices: 155 us -> none  [body(): moved_rows = lax.psum(picked, 'prow')]
    pallas_call x0 -> x1, Pallas kernels: none -> 61.7 us  [fast(): pl.pallas_call(functools.partial(kernel, shape), out_shape=jax.ShapeDtype...]
    dot_general x2 -> x0, matrix products: 15 us -> none  [the longest x1 7.77 us: body(): jnp.dot(l_inverse, moved_rows[:panel_width], precision=lax.Precision.HIGH...]
    scatter x2 -> x0, local copies, waits for them, and re-layouts: 8.64 us -> none  [body(): permuted = matrix.at[target_idx].set(moved_rows, mode='drop')]
    gather x1 -> x0, local copies, waits for them, and re-layouts: 5.24 us -> none  [body(): taken = matrix[jnp.clip(local_idx, 0, row_dev - 1)]]
    select_n x2 -> x1, other arithmetic: 3.85 us -> 0.01 us  [plan(): here = (r - CH * z + 4 * CH) % NB]
    sub x1, local copies, waits for them, and re-layouts: 3.04 us -> 0.01 us  [plan(): near = jnp.where(s < NB // 2, s, NB - 1 - s) // HALF]
    unnamed x9, local copies, waits for them, and re-layouts: 1.86 us -> 4.06 us
  transfers between devices with their start and end apart: 2 -> 0, of which waited for: 1 -> 0; matrix products, arithmetic and copies ran while one was open for 8% -> 0% of each run, Pallas kernels for 0% -> 0%
where the time goes in v1:
time: 71.2 us; the launch traced here: 71 us
  Pallas kernels  61.7 us (87%)
  local copies, waits for them, and re-layouts  5.24 us (7%)
  other arithmetic  3.05 us (4%)
    pallas_call x1, Pallas kernels, fast(): pl.pallas_call(functools.partial(kernel, shape), out_shape=jax.ShapeDtype...  61.7 us
    unnamed x9, local copies, waits for them, and re-layouts  4.06 us
    reduce_sum x1, other arithmetic, place(): jnp.sum(jnp.where(pos[:, None] == idx[None, :], values[:, None], 0), axis=0)  1.7 us

profile of v1, /device:TPU:6, one launch (start us, length us, event | category | flops | bytes accessed | tf_op | source)
XLA Modules:
  0.0 71.0 jit_solution(10276324293679545391)
XLA Ops:
  0.0 0.0 copy-start
  0.0 0.0 copy-start.6
  0.0 0.0 copy-start.8
  0.0 0.0 copy-start.7
  0.0 0.8 %copy-done.8 = s32[1024]{0:T(1024)S(1)} copy-done((s32[1024]{0:T(1024)S(1)}, s32[1024]{0:T(1024)}, u32[]{:S(2)}) %copy-start.8) | copy-done | bytes 4120
  0.9 0.0 copy-done.7
  0.9 0.4 convert_reduce_fusion
  1.3 0.3 fusion.5
  1.5 0.7 and_reduce_fusion.1
  2.9 0.1 lt.130
  3.0 1.1 %lt.131 = s32[512,512]{1,0:T(8,128)} iota(), iota_dimension=0 | iota | bytes 1048576 | tf_op jit(solution)/shard_map/lt | solution.py:277
  4.0 0.0 copy-done
  4.0 0.0 copy-done.6
  4.0 63.7 %conditional.1 = (f32[768,768]{1,0:T(8,128)}) conditional(s32[]{:T(128)} %convert_element_type.11, (s32[1024]{0:T(1024)S(1)}, s32[1024]{0:T(1024)S(1)}, f32[768,768]{1,0:T(8,128)S(1)}, f32[16,768]{1,0:T(8,128)S(1)}, f32[512,512]{1,0:T(8,128)}) %tuple.92, (s32[512]{0:T(512)S(1)}, (), s32[512]{0:T(512)S(1)}, s32[512]{0:T(512)S(1)}, ...), branch_computations={%region_4.0_spmd, %region_11.16_spmd} | conditional | flops 6041991168 | bytes 112721744 | solution.py:373
  4.3 0.0 copy-start.5
  4.3 1.7 %select_reduce_fusion = (s32[512]{0:T(512)S(1)}, s32[512]{0:T(512)S(1)}, s32[512]{0:T(512)S(1)}, s32[512]{0:T(512)S(1)}) fusion(s32[512]{0:T(512)S(1)} %get-tuple-element.250, s32[512]{0:T(512)S(1)} %slice.30, s32[512,512]{1,0:T(8,128)S(1)} %get-tuple-element.247, s32[512]{0:T(512)S(1)} %get-tuple-element.246, s32[512]{0:T(512)S(1)} %get-tuple-element.245, ...), kind=kLoop, calls=%fused_computation.3 | loop fusion | flops 2619392 | bytes 3164160 | tf_op jit(solution)/shard_map/reduce_sum | solution.py:285
  6.0 0.0 copy-done.5
  6.0 61.7 %branch_1_fun.1 = f32[768,768]{1,0:T(8,128)} custom-call(s32[512]{0:T(512)S(1)} %get-tuple-element.286.qsrc, s32[512]{0:T(512)S(1)} %get-tuple-element.267.ssrc, s32[1,512]{1,0:T(1,128)S(1)} %bitcast.15, s32[1,512]{1,0:T(1,128)S(1)} %bitcast.14, f32[768,768]{1,0:T(8,128)S(1)} %get-tuple-element.251.mat, f32[16,768]{1,0:T(8,128)S(1)} %get-tuple-element.252.pan, ...), custom_call_target="tpu_custom_call" | custom-call | tf_op jit(solution)/shard_map/cond/branch_1_fun/pallas_call | solution.py:342
  67.8 3.2 %copy.36 = f32[768,768]{1,0:T(8,128)} copy(f32[768,768]{1,0:T(8,128)} %get-tuple-element.254) | data formatting | bytes 4718592
  (6 shorter events, 0.0 us)
Async XLA Ops:
  0.0 4.0 %copy-start = (f32[768,768]{1,0:T(8,128)S(1)}, f32[768,768]{1,0:T(8,128)}, u32[]{:S(2)}) copy-start(f32[768,768]{1,0:T(8,128)} %param.13) | copy-start | bytes 7077892
  0.0 4.0 %copy-start.6 = (f32[768,16]{0,1:T(8,128)S(1)}, f32[768,16]{0,1:T(8,128)}, u32[]{:S(2)}) copy-start(f32[768,16]{0,1:T(8,128)} %param.14) | copy-start | bytes 147460
  0.0 0.8 %copy-start.8 = (s32[1024]{0:T(1024)S(1)}, s32[1024]{0:T(1024)}, u32[]{:S(2)}) copy-start(s32[1024]{0:T(1024)} %param.16) | copy-start | bytes 12292
  0.0 0.9 %copy-start.7 = (s32[1024]{0:T(1024)S(1)}, s32[1024]{0:T(1024)}, u32[]{:S(2)}) copy-start(s32[1024]{0:T(1024)} %param.17) | copy-start | bytes 12292
  4.3 1.7 %copy-start.5 = (f32[512,512]{1,0:T(8,128)S(1)}, f32[512,512]{1,0:T(8,128)}, u32[]{:S(2)}) copy-start(f32[512,512]{1,0:T(8,128)} %get-tuple-element.253.linv) | copy-start | bytes 3145732 | tf_op jit(solution)/shard_map/cond

commit v2 on v1

v2 whole, which is shorter than its diff:
```python
import functools

import jax
import jax.numpy as jnp
from jax import lax
from jax.experimental import pallas as pl
from jax.experimental.pallas import tpu as pltpu
from jax.sharding import PartitionSpec as P

MESH = pl.DeviceIdType.MESH
NZ = 16
CH = 32
HALF = 16
WIN = 256
NB = NZ * CH
F32, BF16 = jnp.float32, jnp.bfloat16


def reach(j):
    return (j + 1) // 2 + 2


UPWARDS = [(8, 7)] * NZ
KSTEP = max(max(a, NZ - 1 - a) for p in UPWARDS for a in p)
BLOCKS = [2] * 8


def window(z):
    return jnp.clip(2 * z - 7, 0, 16)


def split(x):
    hi = x.astype(BF16)
    return hi, (x - hi.astype(F32)).astype(BF16)


def dot(a, b, ca=1):
    return lax.dot_general(a, b, (((ca,), (0,)), ((), ())), preferred_element_type=F32)


def kernel(
    shape, qsrc, ssrc, inv_ref, tgt_ref, mat_hbm, pan, linv_hbm, out,
    mat, linv, contrib, left1, right1, left2, right2, q, t, pall, lhi, llo, whi, wlo, hot,
    p_send, p_recv, g_send, g_recv, s_send, s_recv, pan_send, pan_recv, load,
):
    ny, nx, nc = shape
    rows, cols = mat.shape
    z = lax.axis_index("prow")
    w = lax.axis_index("pcol")
    core, x, y = w % nc, (w // nc) % nx, w // (nc * nx)
    off = z * rows
    up, down = (z + 1) % NZ, (z + NZ - 1) % NZ
    dist = (z, (NZ - z) % NZ)
    nxt = ({"prow": up}, {"prow": down})

    def pcol(yy, xx, cc):
        return {"pcol": (yy * nx + xx) * nc + cc}

    xpart = [pcol(y, (x + d) % nx, core) for d in range(1, nx)]
    ypart = [pcol((y + d) % ny, x, core) for d in range(1, ny)]
    cpart = [pcol(y, x, 1 - core)] if nc == 2 else []
    partners = list(nxt) + xpart + ypart + cpart
    mine = y * nx + x

    loads = [
        pltpu.make_async_copy(mat_hbm, mat, load.at[0]),
        pltpu.make_async_copy(linv_hbm, linv, load.at[1]),
        pltpu.make_async_copy(pan, pall.at[mine, core], load.at[2]),
    ]
    for c in loads:
        c.start()
    t[...] = jnp.zeros_like(t)

    barrier = pltpu.get_barrier_semaphore()
    for dev in partners:
        pl.semaphore_signal(barrier, inc=1, device_id=dev, device_id_type=MESH)
    pl.semaphore_wait(barrier, len(partners))

    def remote(src, dst, ss, rs, dev):
        return pltpu.make_async_remote_copy(
            src_ref=src, dst_ref=dst, send_sem=ss, recv_sem=rs, device_id=dev, device_id_type=MESH
        )

    def on(devices, act):
        if len(devices) == NZ:
            act()
            return
        starts = [i for i in sorted(devices) if (i - 1) % NZ not in devices]
        hit = None
        for i in starts:
            n = 1
            while (i + n) % NZ in devices:
                n += 1
            one = (z + NZ - i) % NZ < n
            hit = one if hit is None else hit | one
        if hit is not None:
            pl.when(hit)(act)

    def pan_x(i):
        return remote(pan, pall.at[mine, core], pan_send.at[i], pan_recv.at[i], xpart[i])

    def pan_y(i):
        rowset = pall.at[pl.ds(y * nx, nx), core]
        return remote(rowset, rowset, pan_send.at[nx - 1 + i], pan_recv.at[nx - 1 + i], ypart[i])

    def pan_c():
        k = nx + ny - 2
        return remote(pall.at[:, core], pall.at[:, core], pan_send.at[k], pan_recv.at[k], cpart[0])

    def home(d, k):
        if k == 0:
            src = contrib.at[pl.ds(112, HALF)] if d == 0 else contrib.at[pl.ds(0, HALF)]
            dst = (left1, right1)[d]
        else:
            src = contrib.at[pl.ds(80, CH)] if d == 0 else contrib.at[pl.ds(16, CH)]
            dst = (left2, right2)[d]
        i = 2 * k + d
        return remote(src, dst, p_send.at[i], p_recv.at[i], nxt[d])

    def gather(d, k, u):
        src, dst = ((5 - k) % NZ, (4 - k) % NZ) if d == 0 else (3 + k, 4 + k)
        part = pl.ds(HALF * u, HALF)
        i = (2 * (k - 1) + d) * 2 + u
        return remote(q.at[src, part], q.at[dst, part], g_send.at[i], g_recv.at[i], nxt[d])

    def senders(d, k, u):
        keep = set()
        for i in range(NZ):
            h = (i - (k - 1)) % NZ if d == 0 else (i + (k - 1)) % NZ
            far = UPWARDS[h][u] if d == 0 else NZ - 1 - UPWARDS[h][u]
            if k <= far:
                keep.add(i)
        return keep

    def ring(k):
        for u in (0, 1):
            for d in (0, 1):
                if k > 1:
                    came = {(i + (1 if d == 0 else -1)) % NZ for i in senders(d, k - 1, u)}
                    on(came, lambda: gather(d, k - 1, u).wait_recv())
                if k <= KSTEP:
                    on(senders(d, k, u), lambda: gather(d, k, u).start())

    def take_rows(first, count):
        def one(i, _):
            r = first + i
            li = qsrc[80 + r] - off
            row = mat[pl.ds(jnp.clip(li, 0, rows - 1), 1), :]
            contrib[pl.ds(r, 1), :] = jnp.where((li >= 0) & (li < rows), row, 0.0)
            return 0

        lax.fori_loop(0, count, one, 0, unroll=8)

    def piece(d, j):
        return j if d == 0 else 31 - j

    def scatter(d, j):
        c = piece(d, j)
        return remote(t.at[c], t.at[c], s_send.at[d, j], s_recv.at[d, j], nxt[d])

    nblocks = len(BLOCKS)
    first_of = [15 - sum(BLOCKS[:b]) for b in range(nblocks)]

    def fill(b):
        if b >= nblocks:
            return

        @pl.when(z == 0)
        def _():
            for d in (0, 1):
                base = HALF * (first_of[b] - BLOCKS[b] + 1 if d == 0 else 31 - first_of[b])

                def one(i, _):
                    r = base + i
                    row = mat[pl.ds(jnp.clip(ssrc[r], 0, rows - 1), 1), :]
                    t[r // HALF, pl.ds(r % HALF, 1), :] = row
                    return 0

                lax.fori_loop(0, HALF * BLOCKS[b], one, 0, unroll=8)

    def pass_on(step):
        for d in (0, 1):
            b = step - dist[d]
            first, count = jnp.int32(0), jnp.int32(0)
            for i in range(nblocks):
                first = jnp.where(b == i, first_of[i], first)
                count = jnp.where(b == i, BLOCKS[i], count)
            for u in range(max(BLOCKS)):
                j = jnp.clip(first - u, 0, 15)
                valid = u < count

                @pl.when(valid & (dist[d] >= 1) & (dist[d] <= reach(j)))
                def _():
                    scatter(d, j).wait_recv()

                @pl.when(valid & (dist[d] < reach(j)))
                def _():
                    scatter(d, j).start()

    def order():
        loads[1].wait()
        kk = lax.broadcasted_iota(jnp.int32, (NB, NB), 0)
        perm = (kk == inv_ref[...]).astype(F32).astype(BF16)
        hi, lo = split(linv[...])
        lhi[...] = dot(hi, perm).astype(BF16)
        llo[...] = dot(lo, perm).astype(BF16)

    def base():
        for r in range(0, rows, 256):
            qq = lax.broadcasted_iota(jnp.int32, (256, WIN), 0) + r
            hit = (qq + off == tgt_ref[...]).astype(F32)
            hot[pl.ds(r, 256), :] = hit.astype(BF16)
            gone = jnp.max(hit, axis=1, keepdims=True) > 0.0
            top = (lax.broadcasted_iota(jnp.int32, (256, 1), 0) + r < NB) & (z == 0)
            out[pl.ds(r, 256), :] = jnp.where(gone | top, 0.0, mat[pl.ds(r, 256), :])

    def weights(r):
        a = pall[:, :, :, r:r + 256].reshape(NB, 256)
        ahi, alo = split(a)
        acc = dot(ahi, lhi[...], 0) + dot(ahi, llo[...], 0) + dot(alo, lhi[...], 0)
        qq = lax.broadcasted_iota(jnp.int32, (256, NB), 0) + r
        own = (qq == inv_ref[...]) & (z == 0)
        acc = acc - own.astype(F32)
        hi, lo = split(acc)
        whi[pl.ds(r, 256), :] = hi
        wlo[pl.ds(r, 256), :] = lo

    def product(k, c):
        qhi, qlo = split(q[k // CH:k // CH + 8, :, c:c + 256].reshape(256, 256))
        a, b = whi[:, k:k + 256], wlo[:, k:k + 256]
        return dot(a, qhi) + dot(a, qlo) + dot(b, qhi)

    def update(c):
        out[:, c:c + 256] -= product(0, c)

    def finish(c):
        thi, tlo = split(t[pl.ds(window(z), 16), :, c:c + 256].reshape(WIN, 256))
        out[:, c:c + 256] += dot(hot[...], thi) + dot(hot[...], tlo) - product(256, c)

    stripes = list(range(0, cols, 256))
    later = {1: [order], 2: [base]}
    for i in range(3):
        later[3 + i] = [functools.partial(weights, 256 * i)]
    for i, c in enumerate(stripes):
        later[6 + i] = [functools.partial(update, c)]

    for i in range(nx - 1):
        pan_x(i).start()
    loads[0].wait()
    take_rows(0, HALF)
    take_rows(112, HALF)
    home(0, 0).start()
    home(1, 0).start()
    fill(0)
    pass_on(0)
    take_rows(16, CH)
    take_rows(80, CH)

    home(0, 0).wait_recv()
    contrib[pl.ds(80, HALF), :] += left1[...]
    home(0, 1).start()
    home(1, 0).wait_recv()
    contrib[pl.ds(32, HALF), :] += right1[...]
    home(1, 1).start()
    fill(1)
    pass_on(1)
    take_rows(48, CH)
    fill(2)
    loads[2].wait()
    for i in range(nx - 1):
        pan_x(i).wait_recv()
    for i in range(ny - 1):
        pan_y(i).start()

    home(0, 1).wait_recv()
    home(1, 1).wait_recv()
    q[4] = contrib[pl.ds(48, CH), :] + left2[...] + right2[...]
    for k in range(1, KSTEP + 1):
        ring(k)
        pass_on(1 + k)
        fill(2 + k)
        if k == 2:
            for i in range(ny - 1):
                pan_y(i).wait_recv()
            if cpart:
                pan_c().start()
        if k == 3 and cpart:
            pan_c().wait_recv()
        for f in later.pop(k, []):
            f()
    for fs in later.values():
        for f in fs:
            f()
    for step in range(KSTEP + 2, nblocks + 10):
        pass_on(step)
    ring(KSTEP + 1)
    for c in stripes:
        finish(c)

    for d in (0, 1):
        home(d, 0).wait_send()
        home(d, 1).wait_send()
        for k in range(1, KSTEP + 1):
            for u in (0, 1):
                on(senders(d, k, u), lambda: gather(d, k, u).wait_send())

        def sent(j, _):
            @pl.when(dist[d] < reach(j))
            def _():
                scatter(d, j).wait_send()

            return 0

        lax.fori_loop(0, 16, sent, 0)
    for i in range(nx - 1):
        pan_x(i).wait_send()
    for i in range(ny - 1):
        pan_y(i).wait_send()
    if cpart:
        pan_c().wait_send()


def plan(touched, anchor, rows, z):
    idx = jnp.arange(NB, dtype=jnp.int32)
    src, owner = anchor[:NB], anchor[:NB] // rows
    tgt, top = touched[NB:], anchor[NB:]
    dest = tgt // rows

    def rank(group):
        key = group * NB + idx
        return jnp.sum((key[None, :] < key[:, None]).astype(jnp.int32), axis=1)

    def place(pos, values):
        return jnp.sum(jnp.where(pos[:, None] == idx[None, :], values[:, None], 0), axis=0)

    r, s = rank(owner), rank(tgt)
    here = (r - CH * z + 4 * CH) % NB
    one = place(here, src * NB + idx)
    two = place(s, tgt * NB + jnp.clip(top, 0, NB - 1))
    goes = two // NB
    before = jnp.concatenate([jnp.full((1,), -1, jnp.int32), goes[:-1]])
    goes = jnp.where((goes < NB) | (goes == before), -1, goes)
    goes = lax.dynamic_slice_in_dim(goes, HALF * window(z), WIN)

    away = (owner - r // CH + 8) % NZ - 8
    late = r % CH >= HALF
    fits = (jnp.abs(away) <= 1) | ((away == -2) & ~late) | ((away == 2) & late)
    hops = jnp.where(s < NB // 2, dest, NZ - dest)
    near = jnp.where(s < NB // 2, s, NB - 1 - s) // HALF
    inside = s - HALF * window(dest)
    fits &= (tgt < NB) | ((inside >= 0) & (inside < WIN) & ((dest == 0) | (hops <= reach(near))))
    return jnp.all(fits), one // NB, two % NB, one % NB, goes


def plain(matrix, panel_t, l_inverse, touched, anchor):
    rows = matrix.shape[0]
    offset = lax.axis_index("prow") * rows
    local = anchor - offset
    owned = (local >= 0) & (local < rows)
    picked = jnp.where(owned[:, None], matrix[jnp.clip(local, 0, rows - 1)], 0.0)

    def ring(axis, init):
        n = lax.axis_size(axis)
        pairs = [(i, (i + 1) % n) for i in range(n)]
        return n, lambda v: lax.ppermute(v, axis, pairs), init

    n, shift, _ = ring("prow", None)

    def add(_, carry):
        part, total = carry
        part = shift(part)
        return part, total + part

    _, moved = lax.fori_loop(0, n - 1, add, (picked, picked))
    m, shift_p, _ = ring("pcol", None)
    me = lax.axis_index("pcol")
    wide = jnp.zeros((m,) + panel_t.shape, panel_t.dtype).at[me].set(panel_t)

    def put(i, carry):
        part, whole = carry
        return shift_p(part), lax.dynamic_update_index_in_dim(whole, part, (me - 1 - i) % m, 0)

    _, wide = lax.fori_loop(0, m - 1, put, (shift_p(panel_t), wide))
    high = functools.partial(jnp.dot, precision=lax.Precision.HIGHEST, preferred_element_type=F32)
    upper = high(l_inverse, moved[:NB])
    target = touched - offset
    target = jnp.where((target >= 0) & (target < rows), target, rows)
    lands = jnp.full((rows,), -1, jnp.int32).at[target].set(jnp.arange(2 * NB, dtype=jnp.int32), mode="drop")
    permuted = jnp.where((lands >= 0)[:, None], moved[jnp.clip(lands, 0, 2 * NB - 1)], matrix)
    return permuted - high(wide.reshape(NB, rows).T, upper)


def fast(shape, matrix, panel_t, l_inverse, qsrc, ssrc, inv, tgt):
    rows, cols = matrix.shape
    ny, nx, nc = shape
    vmem, smem = pl.BlockSpec(memory_space=pltpu.VMEM), pl.BlockSpec(memory_space=pltpu.SMEM)
    hbm = pl.BlockSpec(memory_space=pl.ANY)
    npan = max(nx + ny - 1, 1)
    dma = pltpu.SemaphoreType.DMA
    return pl.pallas_call(
        functools.partial(kernel, shape),
        out_shape=pltpu.VMEM((rows, cols), F32),
        in_specs=[smem, smem, vmem, vmem, hbm, hbm, hbm],
        out_specs=vmem,
        scratch_shapes=[
            pltpu.VMEM((rows, cols), F32),
            pltpu.VMEM((NB, NB), F32),
            pltpu.VMEM((128, cols), F32),
            pltpu.VMEM((HALF, cols), F32),
            pltpu.VMEM((HALF, cols), F32),
            pltpu.VMEM((CH, cols), F32),
            pltpu.VMEM((CH, cols), F32),
            pltpu.VMEM((NZ, CH, cols), F32),
            pltpu.VMEM((32, HALF, cols), F32),
            pltpu.VMEM((ny * nx, nc, panel_t.shape[0], rows), F32),
            pltpu.VMEM((NB, NB), BF16),
            pltpu.VMEM((NB, NB), BF16),
            pltpu.VMEM((rows, NB), BF16),
            pltpu.VMEM((rows, NB), BF16),
            pltpu.VMEM((rows, WIN), BF16),
            dma((4,)), dma((4,)), dma((4 * KSTEP,)), dma((4 * KSTEP,)),
            dma((2, 16)), dma((2, 16)), dma((npan,)), dma((npan,)), dma((3,)),
        ],
        compiler_params=pltpu.CompilerParams(
            collective_id=0, has_side_effects=True, vmem_limit_bytes=40 * 2**20
        ),
    )(qsrc, ssrc, inv.reshape(1, NB), tgt.reshape(1, WIN), matrix, panel_t, l_inverse)


def body(shape, matrix, panel, l_inverse, touched, anchor):
    z = lax.axis_index("prow")
    fits, qsrc, ssrc, inv, tgt = plan(touched, anchor, matrix.shape[0], z)
    panel_t = panel.T
    done = fast(shape, matrix, panel_t, l_inverse, qsrc, ssrc, inv, tgt)
    return lax.cond(fits, lambda: done, lambda: plain(matrix, panel_t, l_inverse, touched, anchor))


def solution(mesh):
    n = mesh.shape["pcol"]
    shape = (4, 4, 2) if n == 32 else (1, n, 1)
    in_specs = (P("prow", "pcol"), P("prow", "pcol"), P(), P(), P())
    return jax.shard_map(
        functools.partial(body, shape), mesh=mesh, in_specs=in_specs, out_specs=P("prow", "pcol"), check_vma=False
    )
```

time: 71.2 us -> 62.6 us (0.88)
  Pallas kernels: 61.7 us -> 56.5 us
  local copies, waits for them, and re-layouts: 5.24 us -> 1.48 us
    pallas_call x1, Pallas kernels: 61.7 us -> 56.5 us  [fast(): pl.pallas_call(functools.partial(kernel, shape), out_shape=pltpu.VMEM((ro...]
    unnamed x9 -> x1, local copies, waits for them, and re-layouts: 4.06 us -> 1.41 us
    reduce_sum x1, other arithmetic: 1.7 us -> 0.49 us  [place(): jnp.sum(jnp.where(pos[:, None] == idx[None, :], values[:, None], 0), axis=0)]
    lt x2 -> x0, local copies, waits for them, and re-layouts: 1.17 us -> none  [plan(): idx[None, :] < idx[:, None]]
    add x0 -> x1, other arithmetic: none -> 0.78 us  [plan(): two = place(s, tgt * NB + jnp.clip(top, 0, NB - 1))]
where the time goes in v2:
time: 62.6 us; the launch traced here: 62.2 us
  Pallas kernels  56.5 us (90%)
  other arithmetic  3.26 us (5%)
  local copies, waits for them, and re-layouts  1.48 us (2%)
  between operations  0.71 us (1%)
    pallas_call x1, Pallas kernels, fast(): pl.pallas_call(functools.partial(kernel, shape), out_shape=pltpu.VMEM((ro...  56.5 us
    unnamed x1, local copies, waits for them, and re-layouts  1.41 us
    reduce_and x1, other arithmetic, plan(): return (jnp.all(fits), one // NB, two % NB, one % NB, goes)  1.37 us

profile of v2, /device:TPU:6, one launch (start us, length us, event | category | flops | bytes accessed | tf_op | source)
XLA Modules:
  0.0 62.2 jit_solution(5108642486394699591)
XLA Ops:
  0.0 0.8 %clamp_add_fusion = (s32[512]{0:T(512)S(1)}, s32[512]{0:T(512)S(1)}, s32[512]{0:T(512)S(1)}, s32[512]{0:T(512)S(1)}) fusion(s32[1024]{0:T(1024)} %param.17, s32[1024]{0:T(1024)} %param.16), kind=kLoop, calls=%fused_computation.75 | loop fusion | flops 8192 | bytes 14336 | tf_op jit(solution)/shard_map/add | solution.py:339
  0.8 0.2 convert_reduce_fusion
  1.0 0.3 convert_reduce_fusion.1
  1.3 1.4 %and_reduce_fusion.1 = pred[]{:T(512)} fusion(s32[512]{0:T(512)S(1)} %convert_reduce_fusion, s32[512]{0:T(512)S(1)} %convert_reduce_fusion.1, s32[1024]{0:T(1024)} %param.16, s32[1024]{0:T(1024)} %param.17), kind=kLoop, calls=%fused_computation.99 | loop fusion | flops 57343 | bytes 8193 | tf_op jit(solution)/shard_map/reduce_and | solution.py:352
  3.3 0.5 select_reduce_fusion
  3.9 0.1 or_select_fusion
  3.9 0.1 dynamic_slice.3
  4.0 56.5 %shard_map.57 = f32[768,768]{1,0:T(8,128)S(1)} custom-call(s32[512]{0:T(512)S(1)} %add_select_fusion.2.qsrc, s32[512]{0:T(512)S(1)} %get-tuple-element.189.ssrc, s32[1,512]{1,0:T(1,128)S(1)} %and_select_fusion.inv_ref, s32[1,256]{1,0:T(1,128)S(1)} %bitcast.15, f32[768,768]{1,0:T(8,128)} %mat_hbm.1, f32[16,768]{1,0:T(8,128)} %bitcast.16, f32[512,512]{1,0:T(8,128)} %linv_hbm.1), custom_call_target="tpu_custom_call" | custom-call | tf_op jit(solution)/shard_map/pallas_call | solution.py:400
  60.5 0.2 conditional.1
  60.7 1.4 %copy.31 = f32[768,768]{1,0:T(8,128)} copy(f32[768,768]{1,0:T(8,128)S(1)} %get-tuple-element.167) | data formatting | bytes 4718592
  (4 shorter events, 0.0 us)

commit v3 on v2

--- a/solution.py
+++ b/solution.py
@@ -13,6 +13,7 @@
 HALF = 16
 WIN = 256
 NB = NZ * CH
+BITS = 9
 F32, BF16 = jnp.float32, jnp.bfloat16
 
 
@@ -20,9 +21,12 @@
     return (j + 1) // 2 + 2
 
 
-UPWARDS = [(8, 7)] * NZ
+UPWARDS = [
+    (5, 5), (7, 7), (6, 11), (11, 11), (11, 11), (10, 10), (10, 10), (9, 9),
+    (7, 7), (6, 6), (6, 6), (5, 5), (4, 4), (4, 4), (4, 6), (7, 7),
+]
 KSTEP = max(max(a, NZ - 1 - a) for p in UPWARDS for a in p)
-BLOCKS = [2] * 8
+BLOCKS = [0, 1, 1, 1, 1, 2, 2, 2, 2, 2, 2]
 
 
 def window(z):
@@ -39,7 +43,7 @@
 
 
 def kernel(
-    shape, qsrc, ssrc, inv_ref, tgt_ref, mat_hbm, pan, linv_hbm, out,
+    shape, one_smem, two_smem, one_ref, two_ref, tgt_ref, mat_hbm, pan, linv_hbm, out, misfit,
     mat, linv, contrib, left1, right1, left2, right2, q, t, pall, lhi, llo, whi, wlo, hot,
     p_send, p_recv, g_send, g_recv, s_send, s_recv, pan_send, pan_recv, load,
 ):
@@ -144,7 +148,7 @@
     def take_rows(first, count):
         def one(i, _):
             r = first + i
-            li = qsrc[80 + r] - off
+            li = (one_smem[80 + r] >> BITS) - off
             row = mat[pl.ds(jnp.clip(li, 0, rows - 1), 1), :]
             contrib[pl.ds(r, 1), :] = jnp.where((li >= 0) & (li < rows), row, 0.0)
             return 0
@@ -172,7 +176,7 @@
 
                 def one(i, _):
                     r = base + i
-                    row = mat[pl.ds(jnp.clip(ssrc[r], 0, rows - 1), 1), :]
+                    row = mat[pl.ds(jnp.clip(two_smem[r] & (NB - 1), 0, rows - 1), 1), :]
                     t[r // HALF, pl.ds(r % HALF, 1), :] = row
                     return 0
 
@@ -200,7 +204,7 @@
     def order():
         loads[1].wait()
         kk = lax.broadcasted_iota(jnp.int32, (NB, NB), 0)
-        perm = (kk == inv_ref[...]).astype(F32).astype(BF16)
+        perm = (kk == (one_ref[...] & (NB - 1))).astype(F32).astype(BF16)
         hi, lo = split(linv[...])
         lhi[...] = dot(hi, perm).astype(BF16)
         llo[...] = dot(lo, perm).astype(BF16)
@@ -219,7 +223,7 @@
         ahi, alo = split(a)
         acc = dot(ahi, lhi[...], 0) + dot(ahi, llo[...], 0) + dot(alo, lhi[...], 0)
         qq = lax.broadcasted_iota(jnp.int32, (256, NB), 0) + r
-        own = (qq == inv_ref[...]) & (z == 0)
+        own = (qq == (one_ref[...] & (NB - 1))) & (z == 0)
         acc = acc - own.astype(F32)
         hi, lo = split(acc)
         whi[pl.ds(r, 256), :] = hi
@@ -237,8 +241,25 @@
         thi, tlo = split(t[pl.ds(window(z), 16), :, c:c + 256].reshape(WIN, 256))
         out[:, c:c + 256] += dot(hot[...], thi) + dot(hot[...], tlo) - product(256, c)
 
+    def check():
+        i = lax.broadcasted_iota(jnp.int32, (1, NB), 1)
+
+        def block(v):
+            return sum((v >= rows * b).astype(jnp.int32) for b in range(1, NZ))
+
+        away = (block(one_ref[...] >> BITS) - z - i // CH + 2 * NZ + 12) % NZ - 8
+        late = i % CH >= HALF
+        good = (jnp.abs(away) <= 1) | ((away == -2) & ~late) | ((away == 2) & late)
+        tgt = two_ref[...] >> BITS
+        dest = block(tgt)
+        hops = jnp.where(i < NB // 2, dest, NZ - dest)
+        near = jnp.where(i < NB // 2, i, NB - 1 - i) // HALF
+        inside = i - HALF * window(dest)
+        good &= (tgt < NB) | ((inside >= 0) & (inside < WIN) & ((dest == 0) | (hops <= reach(near))))
+        misfit[0] = jnp.max(jnp.where(good, 0, 1))
+
     stripes = list(range(0, cols, 256))
-    later = {1: [order], 2: [base]}
+    later = {1: [order], 2: [base, check]}
     for i in range(3):
         later[3 + i] = [functools.partial(weights, 256 * i)]
     for i, c in enumerate(stripes):
@@ -324,7 +345,6 @@
     idx = jnp.arange(NB, dtype=jnp.int32)
     src, owner = anchor[:NB], anchor[:NB] // rows
     tgt, top = touched[NB:], anchor[NB:]
-    dest = tgt // rows
 
     def rank(group):
         key = group * NB + idx
@@ -337,19 +357,10 @@
     here = (r - CH * z + 4 * CH) % NB
     one = place(here, src * NB + idx)
     two = place(s, tgt * NB + jnp.clip(top, 0, NB - 1))
-    goes = two // NB
+    goes = two >> BITS
     before = jnp.concatenate([jnp.full((1,), -1, jnp.int32), goes[:-1]])
     goes = jnp.where((goes < NB) | (goes == before), -1, goes)
-    goes = lax.dynamic_slice_in_dim(goes, HALF * window(z), WIN)
-
-    away = (owner - r // CH + 8) % NZ - 8
-    late = r % CH >= HALF
-    fits = (jnp.abs(away) <= 1) | ((away == -2) & ~late) | ((away == 2) & late)
-    hops = jnp.where(s < NB // 2, dest, NZ - dest)
-    near = jnp.where(s < NB // 2, s, NB - 1 - s) // HALF
-    inside = s - HALF * window(dest)
-    fits &= (tgt < NB) | ((inside >= 0) & (inside < WIN) & ((dest == 0) | (hops <= reach(near))))
-    return jnp.all(fits), one // NB, two % NB, one % NB, goes
+    return one, two, lax.dynamic_slice_in_dim(goes, HALF * window(z), WIN)
 
 
 def plain(matrix, panel_t, l_inverse, touched, anchor):
@@ -390,7 +401,7 @@
     return permuted - high(wide.reshape(NB, rows).T, upper)
 
 
-def fast(shape, matrix, panel_t, l_inverse, qsrc, ssrc, inv, tgt):
+def fast(shape, matrix, panel_t, l_inverse, one, two, tgt):
     rows, cols = matrix.shape
     ny, nx, nc = shape
     vmem, smem = pl.BlockSpec(memory_space=pltpu.VMEM), pl.BlockSpec(memory_space=pltpu.SMEM)
@@ -399,9 +410,9 @@
     dma = pltpu.SemaphoreType.DMA
     return pl.pallas_call(
         functools.partial(kernel, shape),
-        out_shape=pltpu.VMEM((rows, cols), F32),
-        in_specs=[smem, smem, vmem, vmem, hbm, hbm, hbm],
-        out_specs=vmem,
+        out_shape=(pltpu.VMEM((rows, cols), F32), jax.ShapeDtypeStruct((1,), jnp.int32)),
+        in_specs=[smem, smem, vmem, vmem, vmem, hbm, hbm, hbm],
+        out_specs=(vmem, smem),
         scratch_shapes=[
             pltpu.VMEM((rows, cols), F32),
             pltpu.VMEM((NB, NB), F32),
@@ -422,17 +433,17 @@
             dma((2, 16)), dma((2, 16)), dma((npan,)), dma((npan,)), dma((3,)),
         ],
         compiler_params=pltpu.CompilerParams(
-            collective_id=0, has_side_effects=True, vmem_limit_bytes=40 * 2**20
+            collective_id=0, has_side_effects=True, vmem_limit_bytes=60 * 2**20
         ),
-    )(qsrc, ssrc, inv.reshape(1, NB), tgt.reshape(1, WIN), matrix, panel_t, l_inverse)
+    )(one, two, one.reshape(1, NB), two.reshape(1, NB), tgt.reshape(1, WIN), matrix, panel_t, l_inverse)
 
 
 def body(shape, matrix, panel, l_inverse, touched, anchor):
     z = lax.axis_index("prow")
-    fits, qsrc, ssrc, inv, tgt = plan(touched, anchor, matrix.shape[0], z)
+    one, two, tgt = plan(touched, anchor, matrix.shape[0], z)
     panel_t = panel.T
-    done = fast(shape, matrix, panel_t, l_inverse, qsrc, ssrc, inv, tgt)
-    return lax.cond(fits, lambda: done, lambda: plain(matrix, panel_t, l_inverse, touched, anchor))
+    done, misfit = fast(shape, matrix, panel_t, l_inverse, one, two, tgt)
+    return lax.cond(misfit[0] == 0, lambda: done, lambda: plain(matrix, panel_t, l_inverse, touched, anchor))
 
 
 def solution(mesh):

time: 62.6 us -> 70.4 us (1.12)
  the two profiles are of different devices: /device:TPU:6 before, /device:TPU:32 now
where the time goes in v3:
time: 70.4 us; the launch traced here: 70.2 us
  Pallas kernels  64.7 us (92%)
  other arithmetic  2.46 us (3%)
  local copies, waits for them, and re-layouts  2.07 us (3%)
    pallas_call x1, Pallas kernels, fast(): pl.pallas_call(functools.partial(kernel, shape), out_shape=(pltpu.VMEM((r...  64.7 us
    unnamed x9, local copies, waits for them, and re-layouts  1.42 us

profile of v3, /device:TPU:32, one launch (start us, length us, event | category | flops | bytes accessed | tf_op | source)
XLA Modules:
  0.0 70.2 jit_solution(3792466727502736443)
XLA Ops:
  0.0 0.0 copy-start.3
  0.0 0.0 copy-start.2
  0.0 0.0 copy-start
  0.0 0.8 %iota_add_fusion = (s32[512]{0:T(512)S(1)}, s32[512]{0:T(512)S(1)}, s32[512]{0:T(512)S(1)}, s32[512]{0:T(512)S(1)}) fusion(s32[1024]{0:T(1024)} %param.16, s32[1024]{0:T(1024)} %param.17), kind=kLoop, calls=%fused_computation.32 | loop fusion | flops 8192 | bytes 14336 | tf_op jit(solution)/shard_map/add | solution.py:350
  0.8 0.2 convert_reduce_fusion
  1.1 0.3 convert_reduce_fusion.1
  1.3 1.1 %select_reduce_fusion = (s32[512]{0:T(512)S(1)}, s32[512]{0:T(512)}) fusion(s32[512]{0:T(512)S(1)} %get-tuple-element.189, s32[512]{0:T(512)S(1)} %convert_reduce_fusion, s32[512]{0:T(512)S(1)} %get-tuple-element.191, s32[512]{0:T(512)S(1)} %add_select_fusion), kind=kLoop, calls=%fused_computation.19 | loop fusion | flops 1571840 | bytes 12288 | tf_op jit(solution)/shard_map/reduce_sum | solution.py:354
  2.4 0.0 copy-start.1
  2.4 0.1 or_select_fusion
  2.5 0.6 dynamic_slice.3
  3.1 0.0 copy-done.1
  3.1 64.7 %shard_map.57 = (f32[768,768]{1,0:T(8,128)S(1)}, s32[1]{0:T(128)}) custom-call(s32[512]{0:T(512)} %get-tuple-element.193.one_smem, s32[512]{0:T(512)} %copy-done.1, s32[1,512]{1,0:T(1,128)} %bitcast.20, s32[1,512]{1,0:T(1,128)} %bitcast.19, s32[1,256]{1,0:T(1,128)} %bitcast.22, f32[768,768]{1,0:T(8,128)} %mat_hbm.1, f32[16,768]{1,0:T(8,128)} %bitcast.17, ...), custom_call_target="tpu_custom_call" | custom-call | tf_op jit(solution)/shard_map/pallas_call | solution.py:411
  68.5 0.0 copy-done.3
  68.5 0.0 copy-done.2
  68.5 0.0 copy-done
  68.5 0.2 conditional.1
  68.8 1.4 %copy.31 = f32[768,768]{1,0:T(8,128)} copy(f32[768,768]{1,0:T(8,128)S(1)} %get-tuple-element.171) | data formatting | bytes 4718592
  (2 shorter events, 0.0 us)
Async XLA Ops:
  0.0 68.5 %copy-start.3 = (s32[1024]{0:T(1024)S(1)}, s32[1024]{0:T(1024)}, u32[]{:S(2)}) copy-start(s32[1024]{0:T(1024)} %param.16) | copy-start | bytes 12292
  0.0 68.5 %copy-start.2 = (s32[1024]{0:T(1024)S(1)}, s32[1024]{0:T(1024)}, u32[]{:S(2)}) copy-start(s32[1024]{0:T(1024)} %param.17) | copy-start | bytes 12292
  0.0 68.5 %copy-start = (f32[768,16]{0,1:T(8,128)S(1)}, f32[768,16]{0,1:T(8,128)}, u32[]{:S(2)}) copy-start(f32[768,16]{0,1:T(8,128)} %param.14) | copy-start | bytes 147460
  2.4 0.7 %copy-start.1 = (s32[512]{0:T(512)}, s32[512]{0:T(512)S(1)}, u32[]{:S(2)}) copy-start(s32[512]{0:T(512)S(1)} %get-tuple-element.192.two_smem) | copy-start | bytes 6148

commit v4 on v3

--- a/solution.py
+++ b/solution.py
@@ -21,12 +21,9 @@
     return (j + 1) // 2 + 2
 
 
-UPWARDS = [
-    (5, 5), (7, 7), (6, 11), (11, 11), (11, 11), (10, 10), (10, 10), (9, 9),
-    (7, 7), (6, 6), (6, 6), (5, 5), (4, 4), (4, 4), (4, 6), (7, 7),
-]
+UPWARDS = [(7, 7)] * 5 + [(8, 8)] * 3 + [(7, 7)] * 8
 KSTEP = max(max(a, NZ - 1 - a) for p in UPWARDS for a in p)
-BLOCKS = [0, 1, 1, 1, 1, 2, 2, 2, 2, 2, 2]
+BLOCKS = [2] * 8
 
 
 def window(z):
@@ -43,7 +40,7 @@
 
 
 def kernel(
-    shape, one_smem, two_smem, one_ref, two_ref, tgt_ref, mat_hbm, pan, linv_hbm, out, misfit,
+    shape, one_smem, two_smem, one_ref, two_ref, mat_hbm, pan, linv_hbm, out, misfit,
     mat, linv, contrib, left1, right1, left2, right2, q, t, pall, lhi, llo, whi, wlo, hot,
     p_send, p_recv, g_send, g_recv, s_send, s_recv, pan_send, pan_recv, load,
 ):
@@ -68,12 +65,11 @@
 
     loads = [
         pltpu.make_async_copy(mat_hbm, mat, load.at[0]),
-        pltpu.make_async_copy(linv_hbm, linv, load.at[1]),
-        pltpu.make_async_copy(pan, pall.at[mine, core], load.at[2]),
+        pltpu.make_async_copy(pan, pall.at[mine, core], load.at[1]),
+        pltpu.make_async_copy(linv_hbm, linv, load.at[2]),
     ]
     for c in loads:
         c.start()
-    t[...] = jnp.zeros_like(t)
 
     barrier = pltpu.get_barrier_semaphore()
     for dev in partners:
@@ -202,7 +198,7 @@
                     scatter(d, j).start()
 
     def order():
-        loads[1].wait()
+        loads[2].wait()
         kk = lax.broadcasted_iota(jnp.int32, (NB, NB), 0)
         perm = (kk == (one_ref[...] & (NB - 1))).astype(F32).astype(BF16)
         hi, lo = split(linv[...])
@@ -210,9 +206,14 @@
         llo[...] = dot(lo, perm).astype(BF16)
 
     def base():
+        tgt = two_ref[...] >> BITS
+        i = lax.broadcasted_iota(jnp.int32, (1, NB), 1)
+        again = (tgt == pltpu.roll(tgt, 1, 1)) & (i > 0)
+        tgt = jnp.where(again | (tgt < NB), -1, tgt)
+        tgt = pltpu.roll(tgt, (NB - HALF * window(z)) % NB, 1)[:, :WIN]
         for r in range(0, rows, 256):
             qq = lax.broadcasted_iota(jnp.int32, (256, WIN), 0) + r
-            hit = (qq + off == tgt_ref[...]).astype(F32)
+            hit = (qq + off == tgt).astype(F32)
             hot[pl.ds(r, 256), :] = hit.astype(BF16)
             gone = jnp.max(hit, axis=1, keepdims=True) > 0.0
             top = (lax.broadcasted_iota(jnp.int32, (256, 1), 0) + r < NB) & (z == 0)
@@ -238,7 +239,10 @@
         out[:, c:c + 256] -= product(0, c)
 
     def finish(c):
-        thi, tlo = split(t[pl.ds(window(z), 16), :, c:c + 256].reshape(WIN, 256))
+        i = window(z) + lax.broadcasted_iota(jnp.int32, (WIN, 1), 0) // HALF
+        near = jnp.where(i < 16, i, 31 - i)
+        came = jnp.where(i < 16, dist[0], dist[1]) <= reach(near)
+        thi, tlo = split(jnp.where(came, t[pl.ds(window(z), 16), :, c:c + 256].reshape(WIN, 256), 0.0))
         out[:, c:c + 256] += dot(hot[...], thi) + dot(hot[...], tlo) - product(256, c)
 
     def check():
@@ -276,6 +280,7 @@
     pass_on(0)
     take_rows(16, CH)
     take_rows(80, CH)
+    loads[1].wait()
 
     home(0, 0).wait_recv()
     contrib[pl.ds(80, HALF), :] += left1[...]
@@ -287,7 +292,6 @@
     pass_on(1)
     take_rows(48, CH)
     fill(2)
-    loads[2].wait()
     for i in range(nx - 1):
         pan_x(i).wait_recv()
     for i in range(ny - 1):
@@ -357,10 +361,7 @@
     here = (r - CH * z + 4 * CH) % NB
     one = place(here, src * NB + idx)
     two = place(s, tgt * NB + jnp.clip(top, 0, NB - 1))
-    goes = two >> BITS
-    before = jnp.concatenate([jnp.full((1,), -1, jnp.int32), goes[:-1]])
-    goes = jnp.where((goes < NB) | (goes == before), -1, goes)
-    return one, two, lax.dynamic_slice_in_dim(goes, HALF * window(z), WIN)
+    return one, two
 
 
 def plain(matrix, panel_t, l_inverse, touched, anchor):
@@ -401,7 +402,7 @@
     return permuted - high(wide.reshape(NB, rows).T, upper)
 
 
-def fast(shape, matrix, panel_t, l_inverse, one, two, tgt):
+def fast(shape, matrix, panel_t, l_inverse, one, two):
     rows, cols = matrix.shape
     ny, nx, nc = shape
     vmem, smem = pl.BlockSpec(memory_space=pltpu.VMEM), pl.BlockSpec(memory_space=pltpu.SMEM)
@@ -410,8 +411,8 @@
     dma = pltpu.SemaphoreType.DMA
     return pl.pallas_call(
         functools.partial(kernel, shape),
-        out_shape=(pltpu.VMEM((rows, cols), F32), jax.ShapeDtypeStruct((1,), jnp.int32)),
-        in_specs=[smem, smem, vmem, vmem, vmem, hbm, hbm, hbm],
+        out_shape=(pltpu.VMEM((rows, cols), F32), pltpu.SMEM((1,), jnp.int32)),
+        in_specs=[smem, smem, vmem, vmem, hbm, hbm, hbm],
         out_specs=(vmem, smem),
         scratch_shapes=[
             pltpu.VMEM((rows, cols), F32),
@@ -433,16 +434,16 @@
             dma((2, 16)), dma((2, 16)), dma((npan,)), dma((npan,)), dma((3,)),
         ],
         compiler_params=pltpu.CompilerParams(
-            collective_id=0, has_side_effects=True, vmem_limit_bytes=60 * 2**20
+            collective_id=0, has_side_effects=True, vmem_limit_bytes=40 * 2**20
         ),
-    )(one, two, one.reshape(1, NB), two.reshape(1, NB), tgt.reshape(1, WIN), matrix, panel_t, l_inverse)
+    )(one, two, one.reshape(1, NB), two.reshape(1, NB), matrix, panel_t, l_inverse)
 
 
 def body(shape, matrix, panel, l_inverse, touched, anchor):
     z = lax.axis_index("prow")
-    one, two, tgt = plan(touched, anchor, matrix.shape[0], z)
+    one, two = plan(touched, anchor, matrix.shape[0], z)
     panel_t = panel.T
-    done, misfit = fast(shape, matrix, panel_t, l_inverse, one, two, tgt)
+    done, misfit = fast(shape, matrix, panel_t, l_inverse, one, two)
     return lax.cond(misfit[0] == 0, lambda: done, lambda: plain(matrix, panel_t, l_inverse, touched, anchor))
 
 

time: 70.4 us -> 59.9 us (0.85)
  the two profiles are of different devices: /device:TPU:32 before, /device:TPU:6 now
where the time goes in v4:
time: 59.9 us; the launch traced here: 59.7 us
  Pallas kernels  56.1 us (94%)
  other arithmetic  1.8 us (3%)
  local copies, waits for them, and re-layouts  1.42 us (2%)
    pallas_call x1, Pallas kernels, fast(): pl.pallas_call(functools.partial(kernel, shape), out_shape=(pltpu.VMEM((r...  56.1 us
    unnamed x7, local copies, waits for them, and re-layouts  1.42 us

profile of v4, /device:TPU:6, one launch (start us, length us, event | category | flops | bytes accessed | tf_op | source)
XLA Modules:
  0.0 59.7 jit_solution(4079069859871674105)
XLA Ops:
  0.0 0.0 copy-start.2
  0.0 0.0 copy-start.1
  0.0 0.0 copy-start
  0.0 0.8 %iota_add_fusion = (s32[512]{0:T(512)S(1)}, s32[512]{0:T(512)S(1)}, s32[512]{0:T(512)S(1)}, s32[512]{0:T(512)S(1)}) fusion(s32[1024]{0:T(1024)} %param.16, s32[1024]{0:T(1024)} %param.17), kind=kLoop, calls=%fused_computation.31 | loop fusion | flops 8192 | bytes 14336 | tf_op jit(solution)/shard_map/add | solution.py:354
  0.8 0.2 convert_reduce_fusion
  1.1 0.3 convert_reduce_fusion.1
  1.3 0.5 select_reduce_fusion
  1.8 56.1 %shard_map.57 = (f32[768,768]{1,0:T(8,128)S(1)}, s32[1]{0:T(128)S(4)}) custom-call(s32[512]{0:T(512)S(1)} %get-tuple-element.193.one_smem, s32[512]{0:T(512)S(1)} %get-tuple-element.192.two_smem, s32[1,512]{1,0:T(1,128)S(1)} %bitcast.16, s32[1,512]{1,0:T(1,128)S(1)} %bitcast.15, f32[768,768]{1,0:T(8,128)} %mat_hbm.1, f32[16,768]{1,0:T(8,128)} %bitcast.17, ...), custom_call_target="tpu_custom_call" | custom-call | tf_op jit(solution)/shard_map/pallas_call | solution.py:412
  58.0 0.0 copy-done.2
  58.0 0.0 copy-done.1
  58.0 0.0 copy-done
  58.0 0.2 conditional.1
  58.2 1.4 %copy.31 = f32[768,768]{1,0:T(8,128)} copy(f32[768,768]{1,0:T(8,128)S(1)} %get-tuple-element.171) | data formatting | bytes 4718592
  (1 shorter events, 0.0 us)
Async XLA Ops:
  0.0 58.0 %copy-start.2 = (s32[1024]{0:T(1024)S(1)}, s32[1024]{0:T(1024)}, u32[]{:S(2)}) copy-start(s32[1024]{0:T(1024)} %param.16) | copy-start | bytes 12292
  0.0 58.0 %copy-start.1 = (s32[1024]{0:T(1024)S(1)}, s32[1024]{0:T(1024)}, u32[]{:S(2)}) copy-start(s32[1024]{0:T(1024)} %param.17) | copy-start | bytes 12292
  0.0 58.0 %copy-start = (f32[768,16]{0,1:T(8,128)S(1)}, f32[768,16]{0,1:T(8,128)}, u32[]{:S(2)}) copy-start(f32[768,16]{0,1:T(8,128)} %param.14) | copy-start | bytes 147460

commit v5 on v4

--- a/solution.py
+++ b/solution.py
@@ -21,9 +21,15 @@
     return (j + 1) // 2 + 2
 
 
-UPWARDS = [(7, 7)] * 5 + [(8, 8)] * 3 + [(7, 7)] * 8
-KSTEP = max(max(a, NZ - 1 - a) for p in UPWARDS for a in p)
-BLOCKS = [2] * 8
+UPWARDS = (
+    [(7, 7)] * 5 + [(8, 8)] * 3 + [(7, 7)] * 8,
+    [(8, 8), (10, 10), (10, 10), (7, 10), (10, 10), (10, 10), (9, 9), (8, 8),
+     (8, 8), (7, 7), (5, 5), (5, 5), (5, 5), (5, 6), (6, 6), (7, 7)],
+)
+KSTEP = max(max(a, NZ - 1 - a) for table in UPWARDS for p in table for a in p)
+BLOCKS = ([2] * 8 + [0, 0], [1] * 4 + [2] * 6)
+NBLOCKS = len(BLOCKS[0])
+FIRST = tuple([15 - sum(table[:b]) for b in range(NBLOCKS)] for table in BLOCKS)
 
 
 def window(z):
@@ -81,20 +87,35 @@
             src_ref=src, dst_ref=dst, send_sem=ss, recv_sem=rs, device_id=dev, device_id_type=MESH
         )
 
-    def on(devices, act):
-        if len(devices) == NZ:
-            act()
-            return
-        starts = [i for i in sorted(devices) if (i - 1) % NZ not in devices]
+    def among(devices):
         hit = None
-        for i in starts:
+        for i in sorted(devices):
+            if (i - 1) % NZ in devices:
+                continue
             n = 1
             while (i + n) % NZ in devices:
                 n += 1
             one = (z + NZ - i) % NZ < n
             hit = one if hit is None else hit | one
-        if hit is not None:
+        return hit
+
+    def on(devices, act):
+        sets = [devices(c) for c in range(nc)]
+        if all(len(s) == NZ for s in sets):
+            act()
+        elif all(s == sets[0] for s in sets):
+            if sets[0]:
+                pl.when(among(sets[0]))(act)
+        else:
+            hit = None
+            for c, s in enumerate(sets):
+                if s:
+                    one = core == c if len(s) == NZ else (core == c) & among(s)
+                    hit = one if hit is None else hit | one
             pl.when(hit)(act)
+
+    def by_core(table, b):
+        return jnp.where(core == 0, table[0][b], table[1][b])
 
     def pan_x(i):
         return remote(pan, pall.at[mine, core], pan_send.at[i], pan_recv.at[i], xpart[i])
@@ -123,11 +144,11 @@
         i = (2 * (k - 1) + d) * 2 + u
         return remote(q.at[src, part], q.at[dst, part], g_send.at[i], g_recv.at[i], nxt[d])
 
-    def senders(d, k, u):
+    def senders(d, k, u, c):
         keep = set()
         for i in range(NZ):
             h = (i - (k - 1)) % NZ if d == 0 else (i + (k - 1)) % NZ
-            far = UPWARDS[h][u] if d == 0 else NZ - 1 - UPWARDS[h][u]
+            far = UPWARDS[c][h][u] if d == 0 else NZ - 1 - UPWARDS[c][h][u]
             if k <= far:
                 keep.add(i)
         return keep
@@ -136,10 +157,10 @@
         for u in (0, 1):
             for d in (0, 1):
                 if k > 1:
-                    came = {(i + (1 if d == 0 else -1)) % NZ for i in senders(d, k - 1, u)}
+                    came = lambda c: {(i + (1 if d == 0 else -1)) % NZ for i in senders(d, k - 1, u, c)}
                     on(came, lambda: gather(d, k - 1, u).wait_recv())
                 if k <= KSTEP:
-                    on(senders(d, k, u), lambda: gather(d, k, u).start())
+                    on(functools.partial(senders, d, k, u), lambda: gather(d, k, u).start())
 
     def take_rows(first, count):
         def one(i, _):
@@ -158,34 +179,32 @@
         c = piece(d, j)
         return remote(t.at[c], t.at[c], s_send.at[d, j], s_recv.at[d, j], nxt[d])
 
-    nblocks = len(BLOCKS)
-    first_of = [15 - sum(BLOCKS[:b]) for b in range(nblocks)]
-
     def fill(b):
-        if b >= nblocks:
+        if b >= NBLOCKS or not any(table[b] for table in BLOCKS):
             return
 
         @pl.when(z == 0)
         def _():
-            for d in (0, 1):
-                base = HALF * (first_of[b] - BLOCKS[b] + 1 if d == 0 else 31 - first_of[b])
+            def both(v, _):
+                c = jnp.where(v % 2 == 0, by_core(FIRST, b) - v // 2, 31 - by_core(FIRST, b) + v // 2)
 
                 def one(i, _):
-                    r = base + i
-                    row = mat[pl.ds(jnp.clip(two_smem[r] & (NB - 1), 0, rows - 1), 1), :]
-                    t[r // HALF, pl.ds(r % HALF, 1), :] = row
+                    row = mat[pl.ds(jnp.clip(two_smem[c * HALF + i] & (NB - 1), 0, rows - 1), 1), :]
+                    t[c, pl.ds(i, 1), :] = row
                     return 0
 
-                lax.fori_loop(0, HALF * BLOCKS[b], one, 0, unroll=8)
+                return lax.fori_loop(0, HALF, one, 0, unroll=8)
+
+            lax.fori_loop(0, 2 * by_core(BLOCKS, b), both, 0)
 
     def pass_on(step):
         for d in (0, 1):
             b = step - dist[d]
             first, count = jnp.int32(0), jnp.int32(0)
-            for i in range(nblocks):
-                first = jnp.where(b == i, first_of[i], first)
-                count = jnp.where(b == i, BLOCKS[i], count)
-            for u in range(max(BLOCKS)):
+            for i in range(NBLOCKS):
+                first = jnp.where(b == i, by_core(FIRST, i), first)
+                count = jnp.where(b == i, by_core(BLOCKS, i), count)
+            for u in range(2):
                 j = jnp.clip(first - u, 0, 15)
                 valid = u < count
 
@@ -316,7 +335,7 @@
     for fs in later.values():
         for f in fs:
             f()
-    for step in range(KSTEP + 2, nblocks + 10):
+    for step in range(KSTEP + 2, NBLOCKS + 10):
         pass_on(step)
     ring(KSTEP + 1)
     for c in stripes:
@@ -327,7 +346,7 @@
         home(d, 1).wait_send()
         for k in range(1, KSTEP + 1):
             for u in (0, 1):
-                on(senders(d, k, u), lambda: gather(d, k, u).wait_send())
+                on(functools.partial(senders, d, k, u), lambda: gather(d, k, u).wait_send())
 
         def sent(j, _):
             @pl.when(dist[d] < reach(j))
@@ -449,7 +468,7 @@
 
 def solution(mesh):
     n = mesh.shape["pcol"]
-    shape = (4, 4, 2) if n == 32 else (1, n, 1)
+    shape = (4, 4, 2) if n == 32 else (1, 1, n)
     in_specs = (P("prow", "pcol"), P("prow", "pcol"), P(), P(), P())
     return jax.shard_map(
         functools.partial(body, shape), mesh=mesh, in_specs=in_specs, out_specs=P("prow", "pcol"), check_vma=False

time: 59.9 us -> 61 us (1.018); the launches traced: 59.7 us -> 59.8 us
  no operation moved by 1% of the time
where the time goes in v5:
time: 61 us; the launch traced here: 59.8 us
  Pallas kernels  56.3 us (92%)
  other arithmetic  1.8 us (3%)
  local copies, waits for them, and re-layouts  1.42 us (2%)
    pallas_call x1, Pallas kernels, fast(): pl.pallas_call(functools.partial(kernel, shape), out_shape=(pltpu.VMEM((r...  56.3 us
    unnamed x7, local copies, waits for them, and re-layouts  1.42 us

profile of v5, /device:TPU:6, one launch (start us, length us, event | category | flops | bytes accessed | tf_op | source)
XLA Modules:
  0.0 59.8 jit_solution(9243262753426695860)
XLA Ops:
  0.0 0.0 copy-start.2
  0.0 0.0 copy-start.1
  0.0 0.0 copy-start
  0.0 0.8 %iota_add_fusion = (s32[512]{0:T(512)S(1)}, s32[512]{0:T(512)S(1)}, s32[512]{0:T(512)S(1)}, s32[512]{0:T(512)S(1)}) fusion(s32[1024]{0:T(1024)} %param.16, s32[1024]{0:T(1024)} %param.17), kind=kLoop, calls=%fused_computation.31 | loop fusion | flops 8192 | bytes 14336 | tf_op jit(solution)/shard_map/add | solution.py:373
  0.8 0.2 convert_reduce_fusion
  1.1 0.3 convert_reduce_fusion.1
  1.3 0.5 select_reduce_fusion
  1.8 56.3 %shard_map.57 = (f32[768,768]{1,0:T(8,128)S(1)}, s32[1]{0:T(128)S(4)}) custom-call(s32[512]{0:T(512)S(1)} %get-tuple-element.193.one_smem, s32[512]{0:T(512)S(1)} %get-tuple-element.192.two_smem, s32[1,512]{1,0:T(1,128)S(1)} %bitcast.16, s32[1,512]{1,0:T(1,128)S(1)} %bitcast.15, f32[768,768]{1,0:T(8,128)} %mat_hbm.1, f32[16,768]{1,0:T(8,128)} %bitcast.17, ...), custom_call_target="tpu_custom_call" | custom-call | tf_op jit(solution)/shard_map/pallas_call | solution.py:431
  58.1 0.0 copy-done.2
  58.1 0.0 copy-done.1
  58.1 0.0 copy-done
  58.1 0.2 conditional.1
  58.4 1.4 %copy.31 = f32[768,768]{1,0:T(8,128)} copy(f32[768,768]{1,0:T(8,128)S(1)} %get-tuple-element.171) | data formatting | bytes 4718592
  (1 shorter events, 0.0 us)
Async XLA Ops:
  0.0 58.1 %copy-start.2 = (s32[1024]{0:T(1024)S(1)}, s32[1024]{0:T(1024)}, u32[]{:S(2)}) copy-start(s32[1024]{0:T(1024)} %param.16) | copy-start | bytes 12292
  0.0 58.1 %copy-start.1 = (s32[1024]{0:T(1024)S(1)}, s32[1024]{0:T(1024)}, u32[]{:S(2)}) copy-start(s32[1024]{0:T(1024)} %param.17) | copy-start | bytes 12292
  0.0 58.1 %copy-start = (f32[768,16]{0,1:T(8,128)S(1)}, f32[768,16]{0,1:T(8,128)}, u32[]{:S(2)}) copy-start(f32[768,16]{0,1:T(8,128)} %param.14) | copy-start | bytes 147460

commit v6 on v4

--- a/solution.py
+++ b/solution.py
@@ -41,7 +41,7 @@
 
 def kernel(
     shape, one_smem, two_smem, one_ref, two_ref, mat_hbm, pan, linv_hbm, out, misfit,
-    mat, linv, contrib, left1, right1, left2, right2, q, t, pall, lhi, llo, whi, wlo, hot,
+    mat, linv, contrib, left1, right1, left2, right2, q, t, pall, phi, plo, lhi, llo, whi, wlo, hot,
     p_send, p_recv, g_send, g_recv, s_send, s_recv, pan_send, pan_recv, load,
 ):
     ny, nx, nc = shape
@@ -61,11 +61,11 @@
     ypart = [pcol((y + d) % ny, x, core) for d in range(1, ny)]
     cpart = [pcol(y, x, 1 - core)] if nc == 2 else []
     partners = list(nxt) + xpart + ypart + cpart
-    mine = y * nx + x
+    kd = pan.shape[0]
 
     loads = [
         pltpu.make_async_copy(mat_hbm, mat, load.at[0]),
-        pltpu.make_async_copy(pan, pall.at[mine, core], load.at[1]),
+        pltpu.make_async_copy(pan, pall.at[y, x, core], load.at[1]),
         pltpu.make_async_copy(linv_hbm, linv, load.at[2]),
     ]
     for c in loads:
@@ -96,16 +96,25 @@
         if hit is not None:
             pl.when(hit)(act)
 
-    def pan_x(i):
-        return remote(pan, pall.at[mine, core], pan_send.at[i], pan_recv.at[i], xpart[i])
-
-    def pan_y(i):
-        rowset = pall.at[pl.ds(y * nx, nx), core]
-        return remote(rowset, rowset, pan_send.at[nx - 1 + i], pan_recv.at[nx - 1 + i], ypart[i])
-
-    def pan_c():
-        k = nx + ny - 2
-        return remote(pall.at[:, core], pall.at[:, core], pan_send.at[k], pan_recv.at[k], cpart[0])
+    lanes = ((xpart, ypart), (ypart, xpart))
+    parts = (pl.ds(0, kd // 2), pl.ds(kd // 2, kd // 2))
+
+    def panel(half, step):
+        part = parts[half]
+        copies = []
+        for i, dev in enumerate(lanes[half][step]):
+            if step == 0:
+                src, dst = pan.at[part], pall.at[y, x, core, part]
+            elif half == 0:
+                src = dst = pall.at[y, :, core, part]
+            else:
+                src = dst = pall.at[:, x, core, part]
+            k = (2 * half + step) * 3 + i
+            copies.append(remote(src, dst, pan_send.at[k], pan_recv.at[k], dev))
+        return copies
+
+    def sibling():
+        return remote(pall.at[:, :, core], pall.at[:, :, core], pan_send.at[12], pan_recv.at[12], cpart[0])
 
     def home(d, k):
         if k == 0:
@@ -132,8 +141,10 @@
                 keep.add(i)
         return keep
 
-    def ring(k):
+    def ring(k, between=()):
         for u in (0, 1):
+            for f in between if u == 1 else ():
+                f()
             for d in (0, 1):
                 if k > 1:
                     came = {(i + (1 if d == 0 else -1)) % NZ for i in senders(d, k - 1, u)}
@@ -197,32 +208,32 @@
                 def _():
                     scatter(d, j).start()
 
-    def order():
-        loads[2].wait()
+    def order(dst, low):
         kk = lax.broadcasted_iota(jnp.int32, (NB, NB), 0)
         perm = (kk == (one_ref[...] & (NB - 1))).astype(F32).astype(BF16)
-        hi, lo = split(linv[...])
-        lhi[...] = dot(hi, perm).astype(BF16)
-        llo[...] = dot(lo, perm).astype(BF16)
-
-    def base():
+        dst[...] = dot(split(linv[...])[low], perm).astype(BF16)
+
+    def base(r):
         tgt = two_ref[...] >> BITS
         i = lax.broadcasted_iota(jnp.int32, (1, NB), 1)
         again = (tgt == pltpu.roll(tgt, 1, 1)) & (i > 0)
         tgt = jnp.where(again | (tgt < NB), -1, tgt)
         tgt = pltpu.roll(tgt, (NB - HALF * window(z)) % NB, 1)[:, :WIN]
-        for r in range(0, rows, 256):
-            qq = lax.broadcasted_iota(jnp.int32, (256, WIN), 0) + r
-            hit = (qq + off == tgt).astype(F32)
-            hot[pl.ds(r, 256), :] = hit.astype(BF16)
-            gone = jnp.max(hit, axis=1, keepdims=True) > 0.0
-            top = (lax.broadcasted_iota(jnp.int32, (256, 1), 0) + r < NB) & (z == 0)
-            out[pl.ds(r, 256), :] = jnp.where(gone | top, 0.0, mat[pl.ds(r, 256), :])
+        qq = lax.broadcasted_iota(jnp.int32, (256, WIN), 0) + r
+        hit = (qq + off == tgt).astype(F32)
+        hot[pl.ds(r, 256), :] = hit.astype(BF16)
+        gone = jnp.max(hit, axis=1, keepdims=True) > 0.0
+        top = (lax.broadcasted_iota(jnp.int32, (256, 1), 0) + r < NB) & (z == 0)
+        out[pl.ds(r, 256), :] = jnp.where(gone | top, 0.0, mat[pl.ds(r, 256), :])
+
+    def turn(r):
+        hi, lo = split(pall[:, :, :, :, r:r + 256].reshape(NB, 256).T)
+        phi[pl.ds(r, 256), :] = hi
+        plo[pl.ds(r, 256), :] = lo
 
     def weights(r):
-        a = pall[:, :, :, r:r + 256].reshape(NB, 256)
-        ahi, alo = split(a)
-        acc = dot(ahi, lhi[...], 0) + dot(ahi, llo[...], 0) + dot(alo, lhi[...], 0)
+        ahi, alo = phi[pl.ds(r, 256), :], plo[pl.ds(r, 256), :]
+        acc = dot(ahi, lhi[...]) + dot(ahi, llo[...]) + dot(alo, lhi[...])
         qq = lax.broadcasted_iota(jnp.int32, (256, NB), 0) + r
         own = (qq == (one_ref[...] & (NB - 1))) & (z == 0)
         acc = acc - own.astype(F32)
@@ -263,14 +274,25 @@
         misfit[0] = jnp.max(jnp.where(good, 0, 1))
 
     stripes = list(range(0, cols, 256))
-    later = {1: [order], 2: [base, check]}
-    for i in range(3):
-        later[3 + i] = [functools.partial(weights, 256 * i)]
-    for i, c in enumerate(stripes):
-        later[6 + i] = [functools.partial(update, c)]
-
-    for i in range(nx - 1):
-        pan_x(i).start()
+    call = functools.partial
+    turns, prods, ups = ([call(f, 256 * i) for i in range(3)] for f in (turn, weights, update))
+    bases = [call(base, 256 * i) for i in range(3)]
+    work = {
+        1: ([call(order, llo, 1)], [bases[0]]),
+        2: ([bases[1]], [bases[2], check]),
+        3: ([], []),
+        4: ([], [turns[0]]),
+        5: ([turns[1]], [turns[2], prods[0]]),
+        6: ([prods[1]], [prods[2]]),
+        7: ([ups[0]], [ups[1]]),
+        8: ([ups[2]], []),
+    }
+    if len(stripes) < 3:
+        work[7], work[8] = ([ups[0]], []), ([], [])
+
+    for half in (0, 1):
+        for c in panel(half, 0):
+            c.start()
     loads[0].wait()
     take_rows(0, HALF)
     take_rows(112, HALF)
@@ -281,6 +303,11 @@
     take_rows(16, CH)
     take_rows(80, CH)
     loads[1].wait()
+    for half in (0, 1):
+        for c in panel(half, 0):
+            c.wait_recv()
+        for c in panel(half, 1):
+            c.start()
 
     home(0, 0).wait_recv()
     contrib[pl.ds(80, HALF), :] += left1[...]
@@ -292,29 +319,26 @@
     pass_on(1)
     take_rows(48, CH)
     fill(2)
-    for i in range(nx - 1):
-        pan_x(i).wait_recv()
-    for i in range(ny - 1):
-        pan_y(i).start()
+    loads[2].wait()
+    order(lhi, 0)
 
     home(0, 1).wait_recv()
     home(1, 1).wait_recv()
     q[4] = contrib[pl.ds(48, CH), :] + left2[...] + right2[...]
     for k in range(1, KSTEP + 1):
-        ring(k)
+        between, after = work[k]
+        ring(k, between)
         pass_on(1 + k)
         fill(2 + k)
-        if k == 2:
-            for i in range(ny - 1):
-                pan_y(i).wait_recv()
+        if k == 3:
+            for half in (0, 1):
+                for c in panel(half, 1):
+                    c.wait_recv()
             if cpart:
-                pan_c().start()
-        if k == 3 and cpart:
-            pan_c().wait_recv()
-        for f in later.pop(k, []):
-            f()
-    for fs in later.values():
-        for f in fs:
+                sibling().start()
+        if k == 4 and cpart:
+            sibling().wait_recv()
+        for f in after:
             f()
     for step in range(KSTEP + 2, nblocks + 10):
         pass_on(step)
@@ -337,12 +361,12 @@
             return 0
 
         lax.fori_loop(0, 16, sent, 0)
-    for i in range(nx - 1):
-        pan_x(i).wait_send()
-    for i in range(ny - 1):
-        pan_y(i).wait_send()
+    for half in (0, 1):
+        for step in (0, 1):
+            for c in panel(half, step):
+                c.wait_send()
     if cpart:
-        pan_c().wait_send()
+        sibling().wait_send()
 
 
 def plan(touched, anchor, rows, z):
@@ -407,7 +431,7 @@
     ny, nx, nc = shape
     vmem, smem = pl.BlockSpec(memory_space=pltpu.VMEM), pl.BlockSpec(memory_space=pltpu.SMEM)
     hbm = pl.BlockSpec(memory_space=pl.ANY)
-    npan = max(nx + ny - 1, 1)
+    npan = 13
     dma = pltpu.SemaphoreType.DMA
     return pl.pallas_call(
         functools.partial(kernel, shape),
@@ -424,7 +448,9 @@
             pltpu.VMEM((CH, cols), F32),
             pltpu.VMEM((NZ, CH, cols), F32),
             pltpu.VMEM((32, HALF, cols), F32),
-            pltpu.VMEM((ny * nx, nc, panel_t.shape[0], rows), F32),
+            pltpu.VMEM((ny, nx, nc, panel_t.shape[0], rows), F32),
+            pltpu.VMEM((rows, NB), BF16),
+            pltpu.VMEM((rows, NB), BF16),
             pltpu.VMEM((NB, NB), BF16),
             pltpu.VMEM((NB, NB), BF16),
             pltpu.VMEM((rows, NB), BF16),
@@ -449,7 +475,7 @@
 
 def solution(mesh):
     n = mesh.shape["pcol"]
-    shape = (4, 4, 2) if n == 32 else (1, n, 1)
+    shape = (4, 4, 2) if n == 32 else (1, 1, n)
     in_specs = (P("prow", "pcol"), P("prow", "pcol"), P(), P(), P())
     return jax.shard_map(
         functools.partial(body, shape), mesh=mesh, in_specs=in_specs, out_specs=P("prow", "pcol"), check_vma=False

time: 59.9 us -> 61.1 us (1.020); the launches traced: 59.7 us -> 60.1 us
  no operation moved by 1% of the time
where the time goes in v6:
time: 61.1 us; the launch traced here: 60.1 us
  Pallas kernels  56.5 us (92%)
  other arithmetic  1.8 us (3%)
  local copies, waits for them, and re-layouts  1.42 us (2%)
    pallas_call x1, Pallas kernels, fast(): pl.pallas_call(functools.partial(kernel, shape), out_shape=(pltpu.VMEM((r...  56.5 us
    unnamed x7, local copies, waits for them, and re-layouts  1.42 us

profile of v6, /device:TPU:6, one launch (start us, length us, event | category | flops | bytes accessed | tf_op | source)
XLA Modules:
  0.0 60.1 jit_solution(8116489573923214250)
XLA Ops:
  0.0 0.0 copy-start.2
  0.0 0.0 copy-start.1
  0.0 0.0 copy-start
  0.0 0.8 %iota_add_fusion = (s32[512]{0:T(512)S(1)}, s32[512]{0:T(512)S(1)}, s32[512]{0:T(512)S(1)}, s32[512]{0:T(512)S(1)}) fusion(s32[1024]{0:T(1024)} %param.16, s32[1024]{0:T(1024)} %param.17), kind=kLoop, calls=%fused_computation.31 | loop fusion | flops 8192 | bytes 14336 | tf_op jit(solution)/shard_map/add | solution.py:378
  0.8 0.2 convert_reduce_fusion
  1.1 0.3 convert_reduce_fusion.1
  1.3 0.5 select_reduce_fusion
  1.8 56.5 %shard_map.57 = (f32[768,768]{1,0:T(8,128)S(1)}, s32[1]{0:T(128)S(4)}) custom-call(s32[512]{0:T(512)S(1)} %get-tuple-element.193.one_smem, s32[512]{0:T(512)S(1)} %get-tuple-element.192.two_smem, s32[1,512]{1,0:T(1,128)S(1)} %bitcast.16, s32[1,512]{1,0:T(1,128)S(1)} %bitcast.15, f32[768,768]{1,0:T(8,128)} %mat_hbm.1, f32[16,768]{1,0:T(8,128)} %bitcast.17, ...), custom_call_target="tpu_custom_call" | custom-call | tf_op jit(solution)/shard_map/pallas_call | solution.py:436
  58.4 0.0 copy-done.2
  58.4 0.0 copy-done.1
  58.4 0.0 copy-done
  58.4 0.2 conditional.1
  58.7 1.4 %copy.31 = f32[768,768]{1,0:T(8,128)} copy(f32[768,768]{1,0:T(8,128)S(1)} %get-tuple-element.171) | data formatting | bytes 4718592
  (1 shorter events, 0.0 us)
Async XLA Ops:
  0.0 58.4 %copy-start.2 = (s32[1024]{0:T(1024)S(1)}, s32[1024]{0:T(1024)}, u32[]{:S(2)}) copy-start(s32[1024]{0:T(1024)} %param.16) | copy-start | bytes 12292
  0.0 58.4 %copy-start.1 = (s32[1024]{0:T(1024)S(1)}, s32[1024]{0:T(1024)}, u32[]{:S(2)}) copy-start(s32[1024]{0:T(1024)} %param.17) | copy-start | bytes 12292
  0.0 58.4 %copy-start = (f32[768,16]{0,1:T(8,128)S(1)}, f32[768,16]{0,1:T(8,128)}, u32[]{:S(2)}) copy-start(f32[768,16]{0,1:T(8,128)} %param.14) | copy-start | bytes 147460

commit v7 on v6

--- a/solution.py
+++ b/solution.py
@@ -23,7 +23,7 @@
 
 UPWARDS = [(7, 7)] * 5 + [(8, 8)] * 3 + [(7, 7)] * 8
 KSTEP = max(max(a, NZ - 1 - a) for p in UPWARDS for a in p)
-BLOCKS = [2] * 8
+BLOCKS = [3, 3, 2, 2, 2, 2, 2]
 
 
 def window(z):
@@ -53,6 +53,7 @@
     up, down = (z + 1) % NZ, (z + NZ - 1) % NZ
     dist = (z, (NZ - z) % NZ)
     nxt = ({"prow": up}, {"prow": down})
+    nxt2 = ({"prow": (z + 2) % NZ}, {"prow": (z + NZ - 2) % NZ})
 
     def pcol(yy, xx, cc):
         return {"pcol": (yy * nx + xx) * nc + cc}
@@ -60,7 +61,7 @@
     xpart = [pcol(y, (x + d) % nx, core) for d in range(1, nx)]
     ypart = [pcol((y + d) % ny, x, core) for d in range(1, ny)]
     cpart = [pcol(y, x, 1 - core)] if nc == 2 else []
-    partners = list(nxt) + xpart + ypart + cpart
+    partners = list(nxt) + list(nxt2) + xpart + ypart + cpart
     kd = pan.shape[0]
 
     loads = [
@@ -116,15 +117,15 @@
     def sibling():
         return remote(pall.at[:, :, core], pall.at[:, :, core], pan_send.at[12], pan_recv.at[12], cpart[0])
 
-    def home(d, k):
-        if k == 0:
+    def home(d, far):
+        if far:
             src = contrib.at[pl.ds(112, HALF)] if d == 0 else contrib.at[pl.ds(0, HALF)]
-            dst = (left1, right1)[d]
+            dst, dev = (left1, right1)[d], nxt2[d]
         else:
             src = contrib.at[pl.ds(80, CH)] if d == 0 else contrib.at[pl.ds(16, CH)]
-            dst = (left2, right2)[d]
-        i = 2 * k + d
-        return remote(src, dst, p_send.at[i], p_recv.at[i], nxt[d])
+            dst, dev = (left2, right2)[d], nxt[d]
+        i = 2 * far + d
+        return remote(src, dst, p_send.at[i], p_recv.at[i], dev)
 
     def gather(d, k, u):
         src, dst = ((5 - k) % NZ, (4 - k) % NZ) if d == 0 else (3 + k, 4 + k)
@@ -246,15 +247,15 @@
         a, b = whi[:, k:k + 256], wlo[:, k:k + 256]
         return dot(a, qhi) + dot(a, qlo) + dot(b, qhi)
 
-    def update(c):
-        out[:, c:c + 256] -= product(0, c)
+    def update(k, c):
+        out[:, c:c + 256] -= product(k, c)
 
     def finish(c):
         i = window(z) + lax.broadcasted_iota(jnp.int32, (WIN, 1), 0) // HALF
         near = jnp.where(i < 16, i, 31 - i)
         came = jnp.where(i < 16, dist[0], dist[1]) <= reach(near)
         thi, tlo = split(jnp.where(came, t[pl.ds(window(z), 16), :, c:c + 256].reshape(WIN, 256), 0.0))
-        out[:, c:c + 256] += dot(hot[...], thi) + dot(hot[...], tlo) - product(256, c)
+        out[:, c:c + 256] += dot(hot[...], thi) + dot(hot[...], tlo)
 
     def check():
         i = lax.broadcasted_iota(jnp.int32, (1, NB), 1)
@@ -275,7 +276,7 @@
 
     stripes = list(range(0, cols, 256))
     call = functools.partial
-    turns, prods, ups = ([call(f, 256 * i) for i in range(3)] for f in (turn, weights, update))
+    turns, prods, ups = ([call(f, 256 * i) for i in range(3)] for f in (turn, weights, call(update, 0)))
     bases = [call(base, 256 * i) for i in range(3)]
     work = {
         1: ([call(order, llo, 1)], [bases[0]]),
@@ -295,41 +296,36 @@
             c.start()
     loads[0].wait()
     take_rows(0, HALF)
+    home(1, 1).start()
     take_rows(112, HALF)
+    home(0, 1).start()
+    take_rows(80, CH)
     home(0, 0).start()
+    take_rows(16, CH)
     home(1, 0).start()
     fill(0)
     pass_on(0)
-    take_rows(16, CH)
-    take_rows(80, CH)
+    take_rows(48, CH)
     loads[1].wait()
+    loads[2].wait()
+    fill(1)
     for half in (0, 1):
         for c in panel(half, 0):
             c.wait_recv()
         for c in panel(half, 1):
             c.start()
-
-    home(0, 0).wait_recv()
-    contrib[pl.ds(80, HALF), :] += left1[...]
-    home(0, 1).start()
-    home(1, 0).wait_recv()
-    contrib[pl.ds(32, HALF), :] += right1[...]
-    home(1, 1).start()
-    fill(1)
-    pass_on(1)
-    take_rows(48, CH)
-    fill(2)
-    loads[2].wait()
     order(lhi, 0)
 
-    home(0, 1).wait_recv()
-    home(1, 1).wait_recv()
-    q[4] = contrib[pl.ds(48, CH), :] + left2[...] + right2[...]
+    for d in (0, 1):
+        for far in (0, 1):
+            home(d, far).wait_recv()
+    q[4, 0:HALF] = (contrib[pl.ds(48, HALF), :] + left1[...]) + (left2[0:HALF] + right2[0:HALF])
+    q[4, HALF:CH] = (contrib[pl.ds(64, HALF), :] + right1[...]) + (left2[HALF:CH] + right2[HALF:CH])
     for k in range(1, KSTEP + 1):
         between, after = work[k]
         ring(k, between)
-        pass_on(1 + k)
-        fill(2 + k)
+        pass_on(k)
+        fill(1 + k)
         if k == 3:
             for half in (0, 1):
                 for c in panel(half, 1):
@@ -340,9 +336,11 @@
             sibling().wait_recv()
         for f in after:
             f()
-    for step in range(KSTEP + 2, nblocks + 10):
+    ring(KSTEP + 1)
+    for c in stripes:
+        update(256, c)
+    for step in range(KSTEP + 1, nblocks + 10):
         pass_on(step)
-    ring(KSTEP + 1)
     for c in stripes:
         finish(c)
 

time: 61.1 us -> 60.9 us (level); the launches traced: 60.1 us -> 60.7 us
  Pallas kernels: 56.5 us -> 57.2 us
    pallas_call x1, Pallas kernels: 56.5 us -> 57.2 us  [fast(): pl.pallas_call(functools.partial(kernel, shape), out_shape=(pltpu.VMEM((r...]
where the time goes in v7:
time: 60.9 us; the launch traced here: 60.7 us
  Pallas kernels  57.2 us (94%)
  other arithmetic  1.8 us (3%)
  local copies, waits for them, and re-layouts  1.42 us (2%)
    pallas_call x1, Pallas kernels, fast(): pl.pallas_call(functools.partial(kernel, shape), out_shape=(pltpu.VMEM((r...  57.2 us
    unnamed x7, local copies, waits for them, and re-layouts  1.42 us

profile of v7, /device:TPU:6, one launch (start us, length us, event | category | flops | bytes accessed | tf_op | source)
XLA Modules:
  0.0 60.7 jit_solution(10247997162259599611)
XLA Ops:
  0.0 0.0 copy-start.2
  0.0 0.0 copy-start.1
  0.0 0.0 copy-start
  0.0 0.8 %iota_add_fusion = (s32[512]{0:T(512)S(1)}, s32[512]{0:T(512)S(1)}, s32[512]{0:T(512)S(1)}, s32[512]{0:T(512)S(1)}) fusion(s32[1024]{0:T(1024)} %param.16, s32[1024]{0:T(1024)} %param.17), kind=kLoop, calls=%fused_computation.31 | loop fusion | flops 8192 | bytes 14336 | tf_op jit(solution)/shard_map/add | solution.py:376
  0.8 0.2 convert_reduce_fusion
  1.1 0.3 convert_reduce_fusion.1
  1.3 0.5 select_reduce_fusion
  1.8 57.2 %shard_map.57 = (f32[768,768]{1,0:T(8,128)S(1)}, s32[1]{0:T(128)S(4)}) custom-call(s32[512]{0:T(512)S(1)} %get-tuple-element.193.one_smem, s32[512]{0:T(512)S(1)} %get-tuple-element.192.two_smem, s32[1,512]{1,0:T(1,128)S(1)} %bitcast.16, s32[1,512]{1,0:T(1,128)S(1)} %bitcast.15, f32[768,768]{1,0:T(8,128)} %mat_hbm.1, f32[16,768]{1,0:T(8,128)} %bitcast.17, ...), custom_call_target="tpu_custom_call" | custom-call | tf_op jit(solution)/shard_map/pallas_call | solution.py:434
  59.0 0.0 copy-done.2
  59.1 0.0 copy-done.1
  59.1 0.0 copy-done
  59.1 0.2 conditional.1
  59.3 1.4 %copy.31 = f32[768,768]{1,0:T(8,128)} copy(f32[768,768]{1,0:T(8,128)S(1)} %get-tuple-element.171) | data formatting | bytes 4718592
  (1 shorter events, 0.0 us)
Async XLA Ops:
  0.0 59.0 %copy-start.2 = (s32[1024]{0:T(1024)S(1)}, s32[1024]{0:T(1024)}, u32[]{:S(2)}) copy-start(s32[1024]{0:T(1024)} %param.16) | copy-start | bytes 12292
  0.0 59.1 %copy-start.1 = (s32[1024]{0:T(1024)S(1)}, s32[1024]{0:T(1024)}, u32[]{:S(2)}) copy-start(s32[1024]{0:T(1024)} %param.17) | copy-start | bytes 12292
  0.0 59.1 %copy-start = (f32[768,16]{0,1:T(8,128)S(1)}, f32[768,16]{0,1:T(8,128)}, u32[]{:S(2)}) copy-start(f32[768,16]{0,1:T(8,128)} %param.14) | copy-start | bytes 147460

commit v8 on v7

--- a/solution.py
+++ b/solution.py
@@ -21,9 +21,16 @@
     return (j + 1) // 2 + 2
 
 
-UPWARDS = [(7, 7)] * 5 + [(8, 8)] * 3 + [(7, 7)] * 8
-KSTEP = max(max(a, NZ - 1 - a) for p in UPWARDS for a in p)
-BLOCKS = [3, 3, 2, 2, 2, 2, 2]
+UPWARDS = (
+    [(9, 9), (7, 7), (7, 7), (8, 8), (7, 9), (9, 9), (9, 9), (9, 9),
+     (7, 7), (7, 7), (6, 6), (6, 6), (6, 6), (6, 6), (8, 8), (6, 6)],
+    [(8, 8), (10, 10), (10, 10), (7, 10), (10, 10), (10, 10), (9, 9), (8, 8),
+     (8, 8), (7, 7), (5, 5), (5, 5), (5, 5), (5, 6), (6, 6), (7, 7)],
+)
+KSTEP = max(max(a, NZ - 1 - a) for table in UPWARDS for p in table for a in p)
+BLOCKS = ([2] * 8 + [0], [2, 1, 2, 1, 2, 2, 2, 2, 2])
+NBLOCKS = len(BLOCKS[0])
+FIRST = tuple([15 - sum(table[:b]) for b in range(NBLOCKS)] for table in BLOCKS)
 
 
 def window(z):
@@ -82,20 +89,35 @@
             src_ref=src, dst_ref=dst, send_sem=ss, recv_sem=rs, device_id=dev, device_id_type=MESH
         )
 
-    def on(devices, act):
-        if len(devices) == NZ:
-            act()
-            return
-        starts = [i for i in sorted(devices) if (i - 1) % NZ not in devices]
+    def among(devices):
         hit = None
-        for i in starts:
+        for i in sorted(devices):
+            if (i - 1) % NZ in devices:
+                continue
             n = 1
             while (i + n) % NZ in devices:
                 n += 1
             one = (z + NZ - i) % NZ < n
             hit = one if hit is None else hit | one
-        if hit is not None:
+        return hit
+
+    def on(devices, act):
+        sets = [devices(c) for c in range(nc)]
+        if all(len(s) == NZ for s in sets):
+            act()
+        elif all(s == sets[0] for s in sets):
+            if sets[0]:
+                pl.when(among(sets[0]))(act)
+        else:
+            hit = None
+            for c, s in enumerate(sets):
+                if s:
+                    one = core == c if len(s) == NZ else (core == c) & among(s)
+                    hit = one if hit is None else hit | one
             pl.when(hit)(act)
+
+    def by_core(table, b):
+        return jnp.where(core == 0, table[0][b], table[1][b])
 
     lanes = ((xpart, ypart), (ypart, xpart))
     parts = (pl.ds(0, kd // 2), pl.ds(kd // 2, kd // 2))
@@ -133,11 +155,11 @@
         i = (2 * (k - 1) + d) * 2 + u
         return remote(q.at[src, part], q.at[dst, part], g_send.at[i], g_recv.at[i], nxt[d])
 
-    def senders(d, k, u):
+    def senders(d, k, u, c):
         keep = set()
         for i in range(NZ):
             h = (i - (k - 1)) % NZ if d == 0 else (i + (k - 1)) % NZ
-            far = UPWARDS[h][u] if d == 0 else NZ - 1 - UPWARDS[h][u]
+            far = UPWARDS[c][h][u] if d == 0 else NZ - 1 - UPWARDS[c][h][u]
             if k <= far:
                 keep.add(i)
         return keep
@@ -148,10 +170,10 @@
                 f()
             for d in (0, 1):
                 if k > 1:
-                    came = {(i + (1 if d == 0 else -1)) % NZ for i in senders(d, k - 1, u)}
+                    came = lambda c: {(i + (1 if d == 0 else -1)) % NZ for i in senders(d, k - 1, u, c)}
                     on(came, lambda: gather(d, k - 1, u).wait_recv())
                 if k <= KSTEP:
-                    on(senders(d, k, u), lambda: gather(d, k, u).start())
+                    on(functools.partial(senders, d, k, u), lambda: gather(d, k, u).start())
 
     def take_rows(first, count):
         def one(i, _):
@@ -170,34 +192,32 @@
         c = piece(d, j)
         return remote(t.at[c], t.at[c], s_send.at[d, j], s_recv.at[d, j], nxt[d])
 
-    nblocks = len(BLOCKS)
-    first_of = [15 - sum(BLOCKS[:b]) for b in range(nblocks)]
-
     def fill(b):
-        if b >= nblocks:
+        if b >= NBLOCKS or not any(table[b] for table in BLOCKS):
             return
 
         @pl.when(z == 0)
         def _():
-            for d in (0, 1):
-                base = HALF * (first_of[b] - BLOCKS[b] + 1 if d == 0 else 31 - first_of[b])
+            def both(v, _):
+                c = jnp.where(v % 2 == 0, by_core(FIRST, b) - v // 2, 31 - by_core(FIRST, b) + v // 2)
 
                 def one(i, _):
-                    r = base + i
-                    row = mat[pl.ds(jnp.clip(two_smem[r] & (NB - 1), 0, rows - 1), 1), :]
-                    t[r // HALF, pl.ds(r % HALF, 1), :] = row
+                    row = mat[pl.ds(jnp.clip(two_smem[c * HALF + i] & (NB - 1), 0, rows - 1), 1), :]
+                    t[c, pl.ds(i, 1), :] = row
                     return 0
 
-                lax.fori_loop(0, HALF * BLOCKS[b], one, 0, unroll=8)
+                return lax.fori_loop(0, HALF, one, 0, unroll=8)
+
+            lax.fori_loop(0, 2 * by_core(BLOCKS, b), both, 0)
 
     def pass_on(step):
         for d in (0, 1):
             b = step - dist[d]
             first, count = jnp.int32(0), jnp.int32(0)
-            for i in range(nblocks):
-                first = jnp.where(b == i, first_of[i], first)
-                count = jnp.where(b == i, BLOCKS[i], count)
-            for u in range(max(BLOCKS)):
+            for i in range(NBLOCKS):
+                first = jnp.where(b == i, by_core(FIRST, i), first)
+                count = jnp.where(b == i, by_core(BLOCKS, i), count)
+            for u in range(2):
                 j = jnp.clip(first - u, 0, 15)
                 valid = u < count
 
@@ -322,7 +342,7 @@
     q[4, 0:HALF] = (contrib[pl.ds(48, HALF), :] + left1[...]) + (left2[0:HALF] + right2[0:HALF])
     q[4, HALF:CH] = (contrib[pl.ds(64, HALF), :] + right1[...]) + (left2[HALF:CH] + right2[HALF:CH])
     for k in range(1, KSTEP + 1):
-        between, after = work[k]
+        between, after = work.get(k, ([], []))
         ring(k, between)
         pass_on(k)
         fill(1 + k)
@@ -339,7 +359,7 @@
     ring(KSTEP + 1)
     for c in stripes:
         update(256, c)
-    for step in range(KSTEP + 1, nblocks + 10):
+    for step in range(KSTEP + 1, NBLOCKS + 10):
         pass_on(step)
     for c in stripes:
         finish(c)
@@ -349,7 +369,7 @@
         home(d, 1).wait_send()
         for k in range(1, KSTEP + 1):
             for u in (0, 1):
-                on(senders(d, k, u), lambda: gather(d, k, u).wait_send())
+                on(functools.partial(senders, d, k, u), lambda: gather(d, k, u).wait_send())
 
         def sent(j, _):
             @pl.when(dist[d] < reach(j))

time: 60.9 us -> 63.2 us (1.038)
  Pallas kernels: 57.2 us -> 59.5 us
    pallas_call x1, Pallas kernels: 57.2 us -> 59.5 us  [fast(): pl.pallas_call(functools.partial(kernel, shape), out_shape=(pltpu.VMEM((r...]
where the time goes in v8:
time: 63.2 us; the launch traced here: 63 us
  Pallas kernels  59.5 us (94%)
  other arithmetic  1.8 us (3%)
  local copies, waits for them, and re-layouts  1.42 us (2%)
    pallas_call x1, Pallas kernels, fast(): pl.pallas_call(functools.partial(kernel, shape), out_shape=(pltpu.VMEM((r...  59.5 us
    unnamed x7, local copies, waits for them, and re-layouts  1.42 us

profile of v8, /device:TPU:6, one launch (start us, length us, event | category | flops | bytes accessed | tf_op | source)
XLA Modules:
  0.0 63.0 jit_solution(7961676119341991045)
XLA Ops:
  0.0 0.0 copy-start.2
  0.0 0.0 copy-start.1
  0.0 0.0 copy-start
  0.0 0.8 %iota_add_fusion = (s32[512]{0:T(512)S(1)}, s32[512]{0:T(512)S(1)}, s32[512]{0:T(512)S(1)}, s32[512]{0:T(512)S(1)}) fusion(s32[1024]{0:T(1024)} %param.16, s32[1024]{0:T(1024)} %param.17), kind=kLoop, calls=%fused_computation.31 | loop fusion | flops 8192 | bytes 14336 | tf_op jit(solution)/shard_map/add | solution.py:396
  0.8 0.2 convert_reduce_fusion
  1.1 0.3 convert_reduce_fusion.1
  1.3 0.5 select_reduce_fusion
  1.8 59.5 %shard_map.57 = (f32[768,768]{1,0:T(8,128)S(1)}, s32[1]{0:T(128)S(4)}) custom-call(s32[512]{0:T(512)S(1)} %get-tuple-element.193.one_smem, s32[512]{0:T(512)S(1)} %get-tuple-element.192.two_smem, s32[1,512]{1,0:T(1,128)S(1)} %bitcast.16, s32[1,512]{1,0:T(1,128)S(1)} %bitcast.15, f32[768,768]{1,0:T(8,128)} %mat_hbm.1, f32[16,768]{1,0:T(8,128)} %bitcast.17, ...), custom_call_target="tpu_custom_call" | custom-call | tf_op jit(solution)/shard_map/pallas_call | solution.py:454
  61.3 0.0 copy-done.2
  61.4 0.0 copy-done.1
  61.4 0.0 copy-done
  61.4 0.2 conditional.1
  61.6 1.4 %copy.31 = f32[768,768]{1,0:T(8,128)} copy(f32[768,768]{1,0:T(8,128)S(1)} %get-tuple-element.171) | data formatting | bytes 4718592
  (1 shorter events, 0.0 us)
Async XLA Ops:
  0.0 61.3 %copy-start.2 = (s32[1024]{0:T(1024)S(1)}, s32[1024]{0:T(1024)}, u32[]{:S(2)}) copy-start(s32[1024]{0:T(1024)} %param.16) | copy-start | bytes 12292
  0.0 61.4 %copy-start.1 = (s32[1024]{0:T(1024)S(1)}, s32[1024]{0:T(1024)}, u32[]{:S(2)}) copy-start(s32[1024]{0:T(1024)} %param.17) | copy-start | bytes 12292
  0.0 61.4 %copy-start = (f32[768,16]{0,1:T(8,128)S(1)}, f32[768,16]{0,1:T(8,128)}, u32[]{:S(2)}) copy-start(f32[768,16]{0,1:T(8,128)} %param.14) | copy-start | bytes 147460
